TPU v7x, 128 devices: a whole 4x4x4 slice. The times are simulated.
128 devices in a mesh: ctx: 8 (over y_lo, z), tp: 16 (over x, y_hi, core).
Axes of the slice: x: 4, y: 4 (y_hi: 2, y_lo: 2; y = y_hi * 2 + y_lo), z: 4, core: 2. Of those that a mesh axis runs over, the one named last changes fastest.
Arguments:
- key_feature: bfloat16 [4096, 16384], P('tp', 'ctx'), may hold values from -6 to 6
- value_feature: bfloat16 [4096, 16384], P('tp', 'ctx'), may hold values from -6 to 6
- query_gate: bfloat16 [4096, 16384], P('tp', 'ctx'), may hold values from -6 to 6
- decay_rates: float32 [16, 4096], P(None, 'tp'), may hold values from 1.8310547e-05 to 0.05
- residues: float32 [16, 4096], P(None, 'tp'), may hold values from -4 to 4
- skip_gain: float32 [4096], P('tp'), may hold values from -1 to 1
- out_weight: bfloat16 [4096, 4096], P('tp'), may hold values from -0.125 to 0.125
Outputs:
- mixed_out: bfloat16 [4096, 16384], P('tp', 'ctx')
All inputs are finite; a program needn't handle non-finite values.
Results may differ from a plain program's by a relative error of at most 0.02.
Values may be sent and summed in bfloat16 or wider, within the bound.
A program may use at most 128 MiB of HBM per device.

v0:
```python
import math

import jax
import jax.numpy as jnp
from jax import lax
from jax.sharding import PartitionSpec as P

exact_mode = lax.Precision.HIGHEST


def twiddle_table(row_count, col_count, modulus):
    angle_index = (
        jnp.arange(row_count, dtype=jnp.int32)[:, None]
        * jnp.arange(col_count, dtype=jnp.int32)[None, :]
        % modulus
    )
    angle = angle_index.astype(jnp.float32) * (2.0 * math.pi / modulus)
    return (jnp.cos(angle), jnp.sin(angle))


def split_table(table):
    upper = table.astype(jnp.bfloat16)
    lower = (table - upper.astype(jnp.float32)).astype(jnp.bfloat16)
    return (upper, lower)


def signal_spectrum(signal, outer_tab, mid_tab, inner_tab):
    outer_cos, outer_sin = outer_tab
    mid_cos, mid_sin = mid_tab
    inner_cos, inner_sin = inner_tab
    cos_upper, cos_lower = split_table(outer_cos)
    sin_upper, sin_lower = split_table(outer_sin)
    first_re = jnp.einsum(
        "kn,cnp->ckp", cos_upper, signal, preferred_element_type=jnp.float32
    ) + jnp.einsum("kn,cnp->ckp", cos_lower, signal, preferred_element_type=jnp.float32)
    first_im = -(
        jnp.einsum("kn,cnp->ckp", sin_upper, signal, preferred_element_type=jnp.float32)
        + jnp.einsum("kn,cnp->ckp", sin_lower, signal, preferred_element_type=jnp.float32)
    )
    turned_re = first_re * mid_cos + first_im * mid_sin
    turned_im = first_im * mid_cos - first_re * mid_sin
    final_re = jnp.einsum("ckn,nj->ckj", turned_re, inner_cos, precision=exact_mode) + jnp.einsum(
        "ckn,nj->ckj", turned_im, inner_sin, precision=exact_mode
    )
    final_im = jnp.einsum("ckn,nj->ckj", turned_im, inner_cos, precision=exact_mode) - jnp.einsum(
        "ckn,nj->ckj", turned_re, inner_sin, precision=exact_mode
    )
    return (final_re, final_im)


def taps_spectrum(rates, weights, outer_size, inner_size, seq_length):
    padded_length = 2 * seq_length
    freq = (
        jnp.arange(outer_size, dtype=jnp.int32)[:, None]
        + outer_size * jnp.arange(inner_size, dtype=jnp.int32)[None, :]
    )
    theta = freq.astype(jnp.float32) * (2.0 * math.pi / padded_length)
    parity = 1.0 - 2.0 * (freq % 2).astype(jnp.float32)
    half_sine = jnp.sin(0.5 * theta)
    half_sq = half_sine * half_sine
    full_sine = jnp.sin(theta)
    spec_re = jnp.zeros((rates.shape[1], outer_size, inner_size), jnp.float32)
    spec_im = jnp.zeros((rates.shape[1], outer_size, inner_size), jnp.float32)
    for harmonic in range(rates.shape[0]):
        rate = rates[harmonic][:, None, None]
        amplitude = weights[harmonic][:, None, None] * jnp.sqrt(2.0 * rate / rates.shape[0])
        ratio = jnp.exp(-rate)
        one_minus = -jnp.expm1(-rate)
        tail = jnp.exp(-rate * seq_length)
        numer = (
            amplitude
            * (1.0 - tail * parity[None])
            / (one_minus * one_minus + 4.0 * ratio * half_sq[None])
        )
        spec_re = spec_re + numer * (one_minus + 2.0 * ratio * half_sq[None])
        spec_im = spec_im - numer * ratio * full_sine[None]
    return (spec_re, spec_im)


def inverse_real(spec_re, spec_im, outer_tab, mid_tab, inner_tab, padded_length):
    outer_cos, outer_sin = outer_tab
    mid_cos, mid_sin = mid_tab
    inner_cos, inner_sin = inner_tab
    first_re = jnp.einsum("ckn,nj->ckj", spec_re, inner_cos, precision=exact_mode) - jnp.einsum(
        "ckn,nj->ckj", spec_im, inner_sin, precision=exact_mode
    )
    first_im = jnp.einsum("ckn,nj->ckj", spec_im, inner_cos, precision=exact_mode) + jnp.einsum(
        "ckn,nj->ckj", spec_re, inner_sin, precision=exact_mode
    )
    turned_re = first_re * mid_cos - first_im * mid_sin
    turned_im = first_im * mid_cos + first_re * mid_sin
    result = jnp.einsum("kn,ckp->cnp", outer_cos, turned_re, precision=exact_mode) - jnp.einsum(
        "kn,ckp->cnp", outer_sin, turned_im, precision=exact_mode
    )
    return result / padded_length


def convolve(product, rates, weights, gains):
    seq_length = product.shape[1]
    padded_length = 2 * seq_length
    inner_size = 1
    while inner_size * inner_size < padded_length and padded_length % (2 * inner_size) == 0:
        inner_size = inner_size * 2
    outer_size = padded_length // inner_size
    half_outer = outer_size // 2
    outer_tab = twiddle_table(outer_size, half_outer, outer_size)
    mid_tab = twiddle_table(outer_size, inner_size, padded_length)
    inner_tab = twiddle_table(inner_size, inner_size, inner_size)
    signal_re, signal_im = signal_spectrum(
        product.reshape(-1, half_outer, inner_size), outer_tab, mid_tab, inner_tab
    )
    taps_re, taps_im = taps_spectrum(rates, weights, outer_size, inner_size, seq_length)
    joint_re = signal_re * taps_re - signal_im * taps_im
    joint_im = signal_re * taps_im + signal_im * taps_re
    causal = inverse_real(joint_re, joint_im, outer_tab, mid_tab, inner_tab, padded_length).reshape(
        -1, seq_length
    )
    return causal + gains[:, None] * product.astype(jnp.float32)


def on_device(key_feature, value_feature, query_gate, decay_rates, residues, skip_gain, out_weight):
    product = (key_feature.astype(jnp.float32) * value_feature.astype(jnp.float32)).astype(
        jnp.bfloat16
    )
    owned = product.shape[0] // lax.axis_size("ctx")
    first_row = lax.axis_index("ctx") * owned
    owned_product, owned_gate = (
        lax.all_to_all(product, "ctx", split_axis=0, concat_axis=1, tiled=True),
        lax.all_to_all(query_gate, "ctx", split_axis=0, concat_axis=1, tiled=True),
    )
    rates = lax.dynamic_slice_in_dim(decay_rates, first_row, owned, 1)
    weights = lax.dynamic_slice_in_dim(residues, first_row, owned, 1)
    gains = lax.dynamic_slice_in_dim(skip_gain, first_row, owned, 0)
    filtered = convolve(owned_product, rates, weights, gains)
    owned_gated = (owned_gate.astype(jnp.float32) * filtered).astype(jnp.bfloat16)
    gated = lax.all_to_all(owned_gated, "ctx", split_axis=1, concat_axis=0, tiled=True)
    return lax.psum_scatter(
        lax.dot_general(
            out_weight, gated, (((0,), (0,)), ((), ())), preferred_element_type=jnp.float32
        ).astype(jnp.bfloat16),
        "tp",
        scatter_dimension=0,
        tiled=True,
    )


def solution(mesh):
    in_specs = (
        P("tp", "ctx"),
        P("tp", "ctx"),
        P("tp", "ctx"),
        P(None, "tp"),
        P(None, "tp"),
        P("tp"),
        P("tp", None),
    )
    out_specs = P("tp", "ctx")
    return jax.shard_map(
        on_device, mesh=mesh, in_specs=in_specs, out_specs=out_specs, check_vma=False
    )
```

profile of v0, /device:TPU:1, one launch (start us, length us, event | category | flops | bytes accessed | tf_op | source)
XLA Modules:
  0.0 353.3 jit_solution(9991530588044452334)
XLA Ops:
  6.5 0.0 copy-start
  6.5 3.1 multiply_convert_fusion
  9.6 6.9 %all-to-all-start.1 = ((bf16[8,32,2048]{2,1,0:T(8,128)(2,1)}), bf16[8,32,2048]{2,1,0:T(8,128)(2,1)S(1)}, u32[]{:S(2)}, u32[]{:S(2)}) async-start(bf16[8,32,2048]{2,1,0:T(8,128)(2,1)} %bitcast.326), calls=%async_computation.1 | async-start | bytes 2097152 | tf_op jit(solution)/shard_map/all_to_all | solution.py:128
  16.5 0.5 fusion.62
  17.0 1.7 multiply_sine_fusion
  18.7 1.7 negate_bitcast_fusion.15
  20.4 0.0 copy-start.10
  20.4 0.0 copy-start.11
  20.4 0.0 copy-start.12
  20.4 0.0 copy-start.13
  20.5 0.0 copy-start.14
  20.5 0.0 copy-start.15
  20.5 0.0 copy-start.16
  20.5 0.6 broadcast_multiply_fusion.30
  21.1 0.6 broadcast_multiply_fusion.28
  21.7 0.6 broadcast_multiply_fusion.26
  22.3 0.6 broadcast_multiply_fusion.24
  22.9 0.6 broadcast_multiply_fusion.22
  23.5 0.6 broadcast_multiply_fusion.20
  24.1 1.7 fusion.28.clone.5
  25.8 0.0 copy-done.15
  25.8 0.0 copy-done.16
  25.8 0.0 copy-done.17
  25.9 0.0 copy-done.18
  25.9 0.0 copy-done.19
  25.9 0.0 copy-done.20
  25.9 1.7 copy.27
  27.5 1.7 copy.28
  29.2 0.8 copy.31
  29.9 1.3 dynamic_slice.11
  31.3 0.6 broadcast_multiply_fusion.18
  31.9 1.3 broadcast_multiply_fusion.16
  33.2 1.0 exponential_bitcast_fusion.26
  34.2 1.8 exponential_bitcast_fusion.28
  36.0 0.0 all-to-all-done.1
  36.0 5.2 %all-to-all-start = ((bf16[8,32,2048]{2,1,0:T(8,128)(2,1)}), bf16[8,32,2048]{2,1,0:T(8,128)(2,1)}, u32[]{:S(2)}, u32[]{:S(2)}) async-start(bf16[8,32,2048]{2,1,0:T(8,128)(2,1)} %bitcast.327), calls=%async_computation | async-start | bytes 2097152 | tf_op jit(solution)/shard_map/all_to_all | solution.py:129
  41.2 0.0 reduce-scatter.2.cloned.1.call-start
  41.2 1.5 copy.24
  42.8 2.1 reshape.1212
  44.8 0.8 fusion.78
  45.7 0.8 fusion.76
  46.5 0.9 convolution_add_fusion.2
  47.4 0.9 add_negate_fusion
  48.3 8.4 %fusion.21 = f32[32,128,256]{2,1,0:T(8,128)S(1)} fusion(f32[32,256,128]{2,1,0:T(8,128)S(1)} %add_negate_fusion, f32[32,256,128]{2,1,0:T(8,128)S(1)} %convolution_add_fusion.2, f32[128,256]{0,1:T(8,128)S(1)} %get-tuple-element.225, f32[128,256]{0,1:T(8,128)S(1)} %get-tuple-element.226), kind=kOutput, calls=%fused_computation.51 | convolution fusion | flops 3225288704 | bytes 12845056 | tf_op jit(solution)/shard_map/ckn,nj->ckj/dot_general | solution.py:42
  56.7 8.4 %fusion.17 = f32[32,128,256]{2,1,0:T(8,128)S(1)} fusion(f32[32,256,128]{2,1,0:T(8,128)S(1)} %add_negate_fusion, f32[32,256,128]{2,1,0:T(8,128)S(1)} %convolution_add_fusion.2, f32[128,256]{0,1:T(8,128)S(1)} %get-tuple-element.225, f32[128,256]{0,1:T(8,128)S(1)} %get-tuple-element.226), kind=kOutput, calls=%fused_computation.50 | convolution fusion | flops 3225288704 | bytes 12845056 | tf_op jit(solution)/shard_map/ckn,nj->ckj/dot_general | solution.py:45
  65.5 8.4 %convolution_add_fusion.1 = f32[32,128,256]{2,1,0:T(8,128)S(1)} fusion(f32[32,128,256]{2,1,0:T(8,128)S(1)} %fusion.21, f32[32,256,128]{2,1,0:T(8,128)S(1)} %add_negate_fusion, f32[32,256,128]{2,1,0:T(8,128)S(1)} %convolution_add_fusion.2, f32[128,256]{0,1:T(8,128)S(1)} %get-tuple-element.225, f32[128,256]{0,1:T(8,128)S(1)} %get-tuple-element.226), kind=kOutput, calls=%fused_computation.39 | convolution fusion | flops 3226337280 | bytes 17039360 | tf_op jit(solution)/shard_map/ckn,nj->ckj/dot_general | solution.py:42
  74.3 47.8 %multiply_add_fusion = (f32[32,128,256]{2,1,0:T(8,128)S(1)}, f32[32,128,256]{2,1,0:T(8,128)}, f32[32,128,256]{2,1,0:T(8,128)}, f32[32,128,256]{2,1,0:T(8,128)}) fusion(f32[32,128,256]{2,1,0:T(8,128)S(1)} %convolution_add_fusion.1, f32[32]{0:T(128)} %get-tuple-element.223, f32[32]{0:T(128)S(1)} %copy-done.37, f32[32]{0:T(128)} %get-tuple-element.222, ...), kind=kOutput, calls=%fused_computation.15 | convolution fusion | flops 3445620736 | bytes 34486272 | tf_op jit(solution)/shard_map/ckn,nj->ckj/dot_general | solution.py:45
  122.1 0.0 copy-start.1
  122.1 7.5 %fusion.30 = f32[32,128,256]{1,2,0:T(8,128)} fusion(f32[32,128,256]{2,1,0:T(8,128)S(1)} %get-tuple-element.5), kind=kOutput, calls=%fused_computation.62 | convolution fusion | flops 3222142976 | bytes 8388608 | tf_op jit(solution)/shard_map/ckn,nj->ckj/dot_general | solution.py:87
  129.6 6.3 %multiply_subtract_fusion = f32[32,128,256]{2,1,0:T(8,128)S(1)} fusion(f32[32,128,256]{2,1,0:T(8,128)} %get-tuple-element.224, f32[32,128,256]{2,1,0:T(8,128)} %get-tuple-element.7, f32[32,128,256]{2,1,0:T(8,128)S(1)} %convolution_add_fusion.1, f32[32,128,256]{2,1,0:T(8,128)} %get-tuple-element.6), kind=kLoop, calls=%fused_computation.16 | loop fusion | flops 3145728 | bytes 20971520 | tf_op jit(solution)/shard_map/sub | solution.py:113
  135.9 4.9 %fusion.32 = f32[32,128,256]{1,2,0:T(8,128)S(1)} fusion(f32[32,128,256]{2,1,0:T(8,128)S(1)} %multiply_subtract_fusion), kind=kOutput, calls=%fused_computation.64 | convolution fusion | flops 3222142976 | bytes 8388608 | tf_op jit(solution)/shard_map/ckn,nj->ckj/dot_general | solution.py:84
  140.8 4.9 %convolution_add_fusion = f32[32,128,256]{1,2,0:T(8,128)S(1)} fusion(f32[32,128,256]{1,2,0:T(8,128)S(1)} %copy-done.3, f32[32,128,256]{2,1,0:T(8,128)S(1)} %multiply_subtract_fusion), kind=kOutput, calls=%fused_computation.36 | convolution fusion | flops 3223191552 | bytes 12582912 | tf_op jit(solution)/shard_map/ckn,nj->ckj/dot_general | solution.py:87
  145.7 5.1 %convolution_subtract_fusion = f32[32,128,256]{1,2,0:T(8,128)S(1)} fusion(f32[32,128,256]{1,2,0:T(8,128)S(1)} %fusion.32, f32[32,128,256]{2,1,0:T(8,128)S(1)} %copy-done.2), kind=kOutput, calls=%fused_computation.37 | convolution fusion | flops 3223191552 | bytes 12582912 | tf_op jit(solution)/shard_map/ckn,nj->ckj/dot_general | solution.py:84
  150.8 5.2 %fusion.2 = f32[32,256,64]{1,2,0:T(8,128)S(1)} fusion(f32[32,128,256]{1,2,0:T(8,128)S(1)} %convolution_subtract_fusion, f32[32,128,256]{1,2,0:T(8,128)S(1)} %convolution_add_fusion, f32[128,256]{0,1:T(8,128)S(1)} %get-tuple-element.225, f32[128,256]{0,1:T(8,128)S(1)} %get-tuple-element.226), kind=kOutput, calls=%fused_computation.7 | convolution fusion | flops 808566784 | bytes 10747904 | tf_op jit(solution)/shard_map/kn,ckp->cnp/dot_general | solution.py:92
  156.1 6.8 %multiply_bitcast_fusion = f32[32,64,256]{2,1,0:T(8,128)} fusion(f32[32,256,64]{1,2,0:T(8,128)S(1)} %fusion.2, f32[32,128,256]{1,2,0:T(8,128)S(1)} %convolution_add_fusion, f32[32,128,256]{1,2,0:T(8,128)S(1)} %convolution_subtract_fusion, f32[128,256]{0,1:T(8,128)S(1)} %get-tuple-element.225, f32[128,256]{0,1:T(8,128)S(1)} %get-tuple-element.226), kind=kOutput, calls=%fused_computation.44 | convolution fusion | flops 809615360 | bytes 12845056 | tf_op jit(solution)/shard_map/kn,ckp->cnp/dot_general | solution.py:92
  162.9 2.8 reshape.1213
  165.7 0.0 all-to-all-done
  165.7 0.0 copy-done.56
  165.7 3.2 fusion.10
  168.9 17.9 %all_to_all.45 = bf16[32,8,2048]{2,0,1:T(8,128)(2,1)S(1)} all-to-all(bf16[32,8,2048]{2,0,1:T(8,128)(2,1)S(1)} %fusion.10), channel_id=1, replica_groups=mesh['ctx'=8,'tp'=16] {'ctx'}, dimensions={1} | all-to-all | bytes 2097152 | tf_op jit(solution)/shard_map/all_to_all | solution.py:136
  186.8 8.1 %convert_bitcast_fusion = bf16[4096,2048]{0,1:T(8,128)(2,1)} fusion(bf16[256,2048]{1,0:T(8,128)(2,1)S(1)} %bitcast.325, bf16[256,4096]{1,0:T(8,128)(2,1)S(1)} %copy-done), kind=kOutput, calls=%fused_computation | convolution fusion | flops 4303355904 | bytes 19922944 | tf_op jit(solution)/shard_map/dot_general | solution.py:138
  194.9 0.0 reduce-scatter.2.cloned.1.call-update
  194.9 149.0 %reduce-scatter.2.cloned.1.call-done = bf16[256,2048]{0,1:T(8,128)(2,1)} async-done(((bf16[4096,2048]{0,1:T(8,128)(2,1)}), bf16[256,2048]{0,1:T(8,128)(2,1)}) %reduce-scatter.2.cloned.1.call-update) | async-done | bytes 1048592 | tf_op jit(solution)/shard_map/reduce_scatter | solution.py:137
  343.9 2.3 copy.39
  (99 shorter events, 0.2 us)
Async XLA Ops:
  6.5 180.3 %copy-start = (bf16[256,4096]{1,0:T(8,128)(2,1)S(1)}, bf16[256,4096]{1,0:T(8,128)(2,1)}, u32[]{:S(2)}) copy-start(bf16[256,4096]{1,0:T(8,128)(2,1)} %param.13) | copy-start | bytes 6291460
  9.6 26.4 %all-to-all-start.1 = ((bf16[8,32,2048]{2,1,0:T(8,128)(2,1)}), bf16[8,32,2048]{2,1,0:T(8,128)(2,1)S(1)}, u32[]{:S(2)}, u32[]{:S(2)}) async-start(bf16[8,32,2048]{2,1,0:T(8,128)(2,1)} %bitcast.326), calls=%async_computation.1 | async-start | bytes 2097152 | tf_op jit(solution)/shard_map/all_to_all | solution.py:128
  20.4 3.1 copy-start.10
  20.4 3.7 %copy-start.11 = (f32[1,32]{1,0:T(1,128)}, f32[1,32]{1,0:T(1,128)S(1)}, u32[]{:S(2)}) copy-start(f32[1,32]{1,0:T(1,128)S(1)} %get-tuple-element.53) | copy-start | bytes 388
  20.4 5.4 %copy-start.12 = (f32[1,32]{1,0:T(1,128)}, f32[1,32]{1,0:T(1,128)S(1)}, u32[]{:S(2)}) copy-start(f32[1,32]{1,0:T(1,128)S(1)} %get-tuple-element.55) | copy-start | bytes 388
  20.4 5.4 %copy-start.13 = (f32[1,32]{1,0:T(1,128)}, f32[1,32]{1,0:T(1,128)S(1)}, u32[]{:S(2)}) copy-start(f32[1,32]{1,0:T(1,128)S(1)} %get-tuple-element.69) | copy-start | bytes 388
  20.5 5.4 %copy-start.14 = (f32[1,32]{1,0:T(1,128)}, f32[1,32]{1,0:T(1,128)S(1)}, u32[]{:S(2)}) copy-start(f32[1,32]{1,0:T(1,128)S(1)} %get-tuple-element.9) | copy-start | bytes 388
  20.5 5.4 %copy-start.15 = (f32[1,32]{1,0:T(1,128)}, f32[1,32]{1,0:T(1,128)S(1)}, u32[]{:S(2)}) copy-start(f32[1,32]{1,0:T(1,128)S(1)} %get-tuple-element.57) | copy-start | bytes 388
  20.5 5.4 %copy-start.16 = (f32[1,32]{1,0:T(1,128)}, f32[1,32]{1,0:T(1,128)S(1)}, u32[]{:S(2)}) copy-start(f32[1,32]{1,0:T(1,128)S(1)} %get-tuple-element.59) | copy-start | bytes 388
  20.5 5.4 %copy-start.17 = (f32[1,32]{1,0:T(1,128)}, f32[1,32]{1,0:T(1,128)S(1)}, u32[]{:S(2)}) copy-start(f32[1,32]{1,0:T(1,128)S(1)} %get-tuple-element.61) | copy-start | bytes 388
  20.5 5.4 %copy-start.18 = (f32[1,32]{1,0:T(1,128)}, f32[1,32]{1,0:T(1,128)S(1)}, u32[]{:S(2)}) copy-start(f32[1,32]{1,0:T(1,128)S(1)} %get-tuple-element.63) | copy-start | bytes 388
  20.5 5.4 %copy-start.19 = (f32[1,32]{1,0:T(1,128)}, f32[1,32]{1,0:T(1,128)S(1)}, u32[]{:S(2)}) copy-start(f32[1,32]{1,0:T(1,128)S(1)} %get-tuple-element.65) | copy-start | bytes 388
  20.5 5.4 %copy-start.20 = (f32[1,32]{1,0:T(1,128)}, f32[1,32]{1,0:T(1,128)S(1)}, u32[]{:S(2)}) copy-start(f32[1,32]{1,0:T(1,128)S(1)} %get-tuple-element.67) | copy-start | bytes 388
  36.0 5.2 %copy-start.4 = (bf16[8,32,2048]{2,1,0:T(8,128)(2,1)}, bf16[8,32,2048]{2,1,0:T(8,128)(2,1)S(1)}, u32[]{:S(2)}) copy-start(bf16[8,32,2048]{2,1,0:T(8,128)(2,1)S(1)} %all-to-all-done.1) | copy-start | bytes 3145732
  36.0 129.7 %all-to-all-start = ((bf16[8,32,2048]{2,1,0:T(8,128)(2,1)}), bf16[8,32,2048]{2,1,0:T(8,128)(2,1)}, u32[]{:S(2)}, u32[]{:S(2)}) async-start(bf16[8,32,2048]{2,1,0:T(8,128)(2,1)} %bitcast.327), calls=%async_computation | async-start | bytes 2097152 | tf_op jit(solution)/shard_map/all_to_all | solution.py:129
  41.2 302.8 %reduce-scatter.2.cloned.1.call-start = ((), (), s32[]{:S(2)}) async-start(), calls=%async_computation.4 | async-start | bytes 17825792 | tf_op jit(solution)/shard_map/reduce_scatter | solution.py:137
  65.1 8.8 %copy-start.6 = (f32[256,256,1]{1,0,2:T(8,128)S(1)}, f32[256,256,1]{1,0,2:T(8,128)}, u32[]{:S(2)}) copy-start(f32[256,256,1]{1,0,2:T(8,128)} %fusion.28.clone.5) | copy-start | bytes 786436
  65.1 8.8 %copy-start.7 = (f32[128,256]{1,0:T(8,128)S(1)}, f32[128,256]{1,0:T(8,128)}, u32[]{:S(2)}) copy-start(f32[128,256]{1,0:T(8,128)} %copy.27) | copy-start | bytes 393220
  65.1 8.8 %copy-start.8 = (f32[128,256]{1,0:T(8,128)S(1)}, f32[128,256]{1,0:T(8,128)}, u32[]{:S(2)}) copy-start(f32[128,256]{1,0:T(8,128)} %copy.28) | copy-start | bytes 393220
  65.1 8.8 %copy-start.9 = (f32[128,256]{1,0:T(8,128)S(1)}, f32[128,256]{1,0:T(8,128)}, u32[]{:S(2)}) copy-start(f32[128,256]{1,0:T(8,128)} %copy.31) | copy-start | bytes 393220
  65.2 8.8 %copy-start.21 = (f32[32]{0:T(128)S(1)}, f32[32]{0:T(128)}, u32[]{:S(2)}) copy-start(f32[32]{0:T(128)} %get-tuple-element.8) | copy-start | bytes 388
  65.2 8.8 %copy-start.22 = (f32[32]{0:T(128)S(1)}, f32[32]{0:T(128)}, u32[]{:S(2)}) copy-start(f32[32]{0:T(128)} %get-tuple-element.41) | copy-start | bytes 388
  65.2 8.8 %copy-start.23 = (f32[32]{0:T(128)S(1)}, f32[32]{0:T(128)}, u32[]{:S(2)}) copy-start(f32[32]{0:T(128)} %get-tuple-element.42) | copy-start | bytes 388
  65.2 8.8 %copy-start.24 = (f32[32]{0:T(128)S(1)}, f32[32]{0:T(128)}, u32[]{:S(2)}) copy-start(f32[32]{0:T(128)} %get-tuple-element.44) | copy-start | bytes 388
  65.2 8.8 %copy-start.25 = (f32[32]{0:T(128)S(1)}, f32[32]{0:T(128)}, u32[]{:S(2)}) copy-start(f32[32]{0:T(128)} %get-tuple-element.46) | copy-start | bytes 388
  65.2 8.8 %copy-start.26 = (f32[32]{0:T(128)S(1)}, f32[32]{0:T(128)}, u32[]{:S(2)}) copy-start(f32[32]{0:T(128)} %get-tuple-element.48) | copy-start | bytes 388
  65.2 8.8 %copy-start.27 = (f32[32]{0:T(128)S(1)}, f32[32]{0:T(128)}, u32[]{:S(2)}) copy-start(f32[32]{0:T(128)} %get-tuple-element.50) | copy-start | bytes 388
  65.2 8.8 %copy-start.28 = (f32[32]{0:T(128)S(1)}, f32[32]{0:T(128)}, u32[]{:S(2)}) copy-start(f32[32]{0:T(128)} %get-tuple-element.52) | copy-start | bytes 388
  65.2 8.8 %copy-start.29 = (f32[32]{0:T(128)S(1)}, f32[32]{0:T(128)}, u32[]{:S(2)}) copy-start(f32[32]{0:T(128)} %get-tuple-element.54) | copy-start | bytes 388
  65.2 8.8 %copy-start.30 = (f32[32]{0:T(128)S(1)}, f32[32]{0:T(128)}, u32[]{:S(2)}) copy-start(f32[32]{0:T(128)} %get-tuple-element.56) | copy-start | bytes 388
  65.3 8.8 %copy-start.31 = (f32[32]{0:T(128)S(1)}, f32[32]{0:T(128)}, u32[]{:S(2)}) copy-start(f32[32]{0:T(128)} %get-tuple-element.58) | copy-start | bytes 388
  65.3 8.8 %copy-start.32 = (f32[32]{0:T(128)S(1)}, f32[32]{0:T(128)}, u32[]{:S(2)}) copy-start(f32[32]{0:T(128)} %get-tuple-element.60) | copy-start | bytes 388
  65.3 8.8 %copy-start.33 = (f32[32]{0:T(128)S(1)}, f32[32]{0:T(128)}, u32[]{:S(2)}) copy-start(f32[32]{0:T(128)} %get-tuple-element.62) | copy-start | bytes 388
  65.3 8.8 %copy-start.34 = (f32[32]{0:T(128)S(1)}, f32[32]{0:T(128)}, u32[]{:S(2)}) copy-start(f32[32]{0:T(128)} %get-tuple-element.64) | copy-start | bytes 388
  65.3 8.8 %copy-start.35 = (f32[32]{0:T(128)S(1)}, f32[32]{0:T(128)}, u32[]{:S(2)}) copy-start(f32[32]{0:T(128)} %get-tuple-element.66) | copy-start | bytes 388
  65.3 8.8 %copy-start.36 = (f32[32]{0:T(128)S(1)}, f32[32]{0:T(128)}, u32[]{:S(2)}) copy-start(f32[32]{0:T(128)} %get-tuple-element.68) | copy-start | bytes 388
  65.3 8.8 %copy-start.37 = (f32[32]{0:T(128)S(1)}, f32[32]{0:T(128)}, u32[]{:S(2)}) copy-start(f32[32]{0:T(128)} %get-tuple-element.70) | copy-start | bytes 388
  65.3 8.8 %copy-start.38 = (f32[32]{0:T(128)S(1)}, f32[32]{0:T(128)}, u32[]{:S(2)}) copy-start(f32[32]{0:T(128)} %get-tuple-element.133) | copy-start | bytes 388
  65.3 8.8 %copy-start.39 = (f32[32]{0:T(128)S(1)}, f32[32]{0:T(128)}, u32[]{:S(2)}) copy-start(f32[32]{0:T(128)} %get-tuple-element.134) | copy-start | bytes 388
  65.3 8.8 %copy-start.40 = (f32[32]{0:T(128)S(1)}, f32[32]{0:T(128)}, u32[]{:S(2)}) copy-start(f32[32]{0:T(128)} %get-tuple-element.135) | copy-start | bytes 388
  65.4 8.8 %copy-start.41 = (f32[32]{0:T(128)S(1)}, f32[32]{0:T(128)}, u32[]{:S(2)}) copy-start(f32[32]{0:T(128)} %get-tuple-element.136) | copy-start | bytes 388
  65.4 8.8 %copy-start.42 = (f32[32]{0:T(128)S(1)}, f32[32]{0:T(128)}, u32[]{:S(2)}) copy-start(f32[32]{0:T(128)} %get-tuple-element.137) | copy-start | bytes 388
  65.4 8.8 %copy-start.43 = (f32[32]{0:T(128)S(1)}, f32[32]{0:T(128)}, u32[]{:S(2)}) copy-start(f32[32]{0:T(128)} %get-tuple-element.138) | copy-start | bytes 388
  65.4 8.8 %copy-start.44 = (f32[32]{0:T(128)S(1)}, f32[32]{0:T(128)}, u32[]{:S(2)}) copy-start(f32[32]{0:T(128)} %get-tuple-element.139) | copy-start | bytes 388
  65.4 8.8 %copy-start.45 = (f32[32]{0:T(128)S(1)}, f32[32]{0:T(128)}, u32[]{:S(2)}) copy-start(f32[32]{0:T(128)} %get-tuple-element.140) | copy-start | bytes 388
  65.4 8.8 %copy-start.46 = (f32[32]{0:T(128)S(1)}, f32[32]{0:T(128)}, u32[]{:S(2)}) copy-start(f32[32]{0:T(128)} %get-tuple-element.141) | copy-start | bytes 388
  65.4 8.8 %copy-start.47 = (f32[32]{0:T(128)S(1)}, f32[32]{0:T(128)}, u32[]{:S(2)}) copy-start(f32[32]{0:T(128)} %get-tuple-element.142) | copy-start | bytes 388
  65.4 8.8 %copy-start.48 = (f32[32]{0:T(128)S(1)}, f32[32]{0:T(128)}, u32[]{:S(2)}) copy-start(f32[32]{0:T(128)} %get-tuple-element.143) | copy-start | bytes 388
  65.4 8.8 %copy-start.49 = (f32[32]{0:T(128)S(1)}, f32[32]{0:T(128)}, u32[]{:S(2)}) copy-start(f32[32]{0:T(128)} %get-tuple-element.144) | copy-start | bytes 388
  65.4 8.8 %copy-start.50 = (f32[32]{0:T(128)S(1)}, f32[32]{0:T(128)}, u32[]{:S(2)}) copy-start(f32[32]{0:T(128)} %get-tuple-element.145) | copy-start | bytes 388
  65.5 8.8 %copy-start.51 = (f32[32]{0:T(128)S(1)}, f32[32]{0:T(128)}, u32[]{:S(2)}) copy-start(f32[32]{0:T(128)} %get-tuple-element.146) | copy-start | bytes 388
  65.5 8.8 %copy-start.52 = (f32[32]{0:T(128)S(1)}, f32[32]{0:T(128)}, u32[]{:S(2)}) copy-start(f32[32]{0:T(128)} %get-tuple-element.147) | copy-start | bytes 388
  65.5 8.8 %copy-start.53 = (f32[32]{0:T(128)S(1)}, f32[32]{0:T(128)}, u32[]{:S(2)}) copy-start(f32[32]{0:T(128)} %get-tuple-element.148) | copy-start | bytes 388
  65.5 8.8 %copy-start.54 = (f32[32]{0:T(128)S(1)}, f32[32]{0:T(128)}, u32[]{:S(2)}) copy-start(f32[32]{0:T(128)} %get-tuple-element.149) | copy-start | bytes 388
  65.5 8.8 %copy-start.55 = (f32[32]{0:T(128)S(1)}, f32[32]{0:T(128)}, u32[]{:S(2)}) copy-start(f32[32]{0:T(128)} %get-tuple-element.150) | copy-start | bytes 388
  122.1 7.5 %copy-start.1 = (f32[32,128,256]{2,1,0:T(8,128)}, f32[32,128,256]{2,1,0:T(8,128)S(1)}, u32[]{:S(2)}) copy-start(f32[32,128,256]{2,1,0:T(8,128)S(1)} %get-tuple-element.5) | copy-start | bytes 12582916
  135.9 4.9 %copy-start.3 = (f32[32,128,256]{1,2,0:T(8,128)S(1)}, f32[32,128,256]{1,2,0:T(8,128)}, u32[]{:S(2)}) copy-start(f32[32,128,256]{1,2,0:T(8,128)} %fusion.30) | copy-start | bytes 12582916
  140.8 4.9 %copy-start.2 = (f32[32,128,256]{2,1,0:T(8,128)S(1)}, f32[32,128,256]{2,1,0:T(8,128)}, u32[]{:S(2)}) copy-start(f32[32,128,256]{2,1,0:T(8,128)} %copy-done.1) | copy-start | bytes 12582916
  162.9 2.8 copy-start.5
  162.9 2.8 copy-start.56
Sparse Core Ops, SparseCore 0:
  195.1 148.8 reduce-scatter.1
where the time goes:
time: 358 us; the launch traced here: 353 us
  waiting for transfers between devices  149 us (42%)
  matrix products  119 us (33%)
  other arithmetic  26.4 us (7%)
  blocking collectives  17.9 us (5%)
  between operations  14.6 us (4%)
  local copies, waits for them, and re-layouts  14.3 us (4%)
  starting transfers between devices  12.1 us (3%)
    reduce_scatter x1, waiting for transfers between devices, on_device(): lax.psum_scatter(lax.dot_general(out_weight, gated, (((0,), (0,)), ((), (...  149 us
    dot_general x1, matrix products, signal_spectrum(): jnp.einsum('ckn,nj->ckj', turned_re, inner_sin, precision=exact_mode)  47.8 us
    all_to_all x1, blocking collectives, on_device(): lax.all_to_all(owned_gated, 'ctx', split_axis=1, concat_axis=0, tiled=True)  17.9 us
    dot_general x1, matrix products, signal_spectrum(): jnp.einsum('ckn,nj->ckj', turned_im, inner_cos, precision=exact_mode)  8.44 us
    dot_general x1, matrix products, signal_spectrum(): jnp.einsum('ckn,nj->ckj', turned_im, inner_sin, precision=exact_mode)  8.41 us
    dot_general x1, matrix products, signal_spectrum(): jnp.einsum('ckn,nj->ckj', turned_re, inner_cos, precision=exact_mode)  8.35 us
    dot_general x1, matrix products, on_device(): lax.dot_general(out_weight, gated, (((0,), (0,)), ((), ())), preferred_el...  8.12 us
    dot_general x1, matrix products, inverse_real(): jnp.einsum('ckn,nj->ckj', spec_im, inner_cos, precision=exact_mode)  7.53 us
  transfers between devices with their start and end apart: 3, of which 1 were waited for; matrix products, arithmetic and copies ran while one was open for 40% of the time, Pallas kernels for 0%

commit v1 on v0

v1 whole, which is shorter than its diff:
```python
import functools

import jax
import jax.numpy as jnp
from jax import lax
from jax.experimental import pallas as pl
from jax.experimental.pallas import tpu as pltpu
from jax.sharding import PartitionSpec as P

MESH = pl.DeviceIdType.MESH

MODES = 16
CH = 256
TOK = 2048
CHUNK = 256
NC = TOK // CHUNK
SUB = 32
LANES = 128
CTX = 8
NX = 4
SLOTS = 8

XP, XM, CO, F0, F1, CXM, CXP, C0, C1, YY = range(10)
LAG_FWD, LAG_OPP, LAG_MM, LAG_FIN = 1, 2, 3, 5


def kernel(
    key_hbm, val_hbm, gate_hbm, rate_ref, res_ref, skip_ref, w_hbm, out_hbm,
    keyb, valb, gateb, xt, est, gtot, am1, am2, am4, apow, coef, carry, fr,
    g, w, wt, pself, ysend, yrecv, ostage,
    in_sem, out_sem, ss, rs, fss, frs, wss, wrs,
):
    ctx = lax.axis_index("ctx")
    tp = lax.axis_index("tp")
    x = tp // 4
    yh = (tp // 2) % 2
    core = tp % 2

    def dev(dx, dy, dc):
        return (ctx, ((x + dx) % NX) * 4 + ((yh + dy) % 2) * 2 + (core + dc) % 2)

    def peer(d):
        return ((ctx + d) % CTX, tp)

    x_next, x_prev, other, y_dev = dev(1, 0, 0), dev(3, 0, 0), dev(0, 0, 1), dev(0, 1, 0)
    plane = [(dx, dc) for dx in range(NX) for dc in range(2) if (dx, dc) != (0, 0)]

    barrier = pltpu.get_barrier_semaphore()
    for dx, dc in plane:
        pl.semaphore_signal(barrier, inc=1, device_id=dev(dx, 0, dc), device_id_type=MESH)
    pl.semaphore_signal(barrier, inc=1, device_id=y_dev, device_id_type=MESH)
    for d in range(1, CTX):
        pl.semaphore_signal(barrier, inc=1, device_id=peer(d), device_id_type=MESH)

    loads = [
        pltpu.make_async_copy(key_hbm, keyb, in_sem.at[0]),
        pltpu.make_async_copy(val_hbm, valb, in_sem.at[1]),
        pltpu.make_async_copy(gate_hbm, gateb, in_sem.at[2]),
    ]
    for c in loads:
        c.start()

    def slot_of(dx, dc):
        return ((x + dx) % NX) * 2 + (core + dc) % 2

    me_slot = slot_of(0, 0)

    def w_cols(dx, dc, yb):
        col = (((x + dx) % NX) * 4 + yb * 2 + (core + dc) % 2) * CH
        return w_hbm.at[:, pl.ds(pl.multiple_of(col, CH), CH)]

    own_w = [
        pltpu.make_async_copy(w_cols(0, 0, yb), w.at[me_slot, yb], in_sem.at[3 + yb]) for yb in range(2)
    ]
    for c in own_w:
        c.start()

    pl.semaphore_wait(barrier, len(plane) + 1 + CTX - 1)

    def w_copy(dx, dc, yb, slot):
        i = dx * 2 + dc
        return pltpu.make_async_remote_copy(
            w_cols(dx, dc, yb), w.at[slot, yb], wss.at[i, yb], wrs.at[i, yb],
            device_id=dev(dx, 0, dc), device_id_type=MESH,
        )

    for dx, dc in plane:
        for yb in range(2):
            w_copy(dx, dc, yb, me_slot).start()

    rate = rate_ref[...]
    for m in range(MODES):
        r8 = jnp.broadcast_to(rate[m : m + 1, :], (8, CH))
        sub = lax.broadcasted_iota(jnp.int32, (8, CH), 0)
        subf = sub.astype(jnp.float32)
        am1[m] = jnp.where(sub >= 1, jnp.exp(-r8 * float(SUB)), 0.0)
        am2[m] = jnp.where(sub >= 2, jnp.exp(-r8 * float(2 * SUB)), 0.0)
        am4[m] = jnp.where(sub >= 4, jnp.exp(-r8 * float(4 * SUB)), 0.0)
        apow[m] = jnp.exp(-r8 * (subf * float(SUB)))
    coef[0] = jnp.exp(-rate)
    coef[1] = res_ref[...] * jnp.sqrt(2.0 * rate / MODES)
    coef[2] = jnp.exp(-rate * float(CHUNK))

    loads[0].wait()
    loads[1].wait()

    def pass1(n, c0):
        ts = pl.ds(pl.multiple_of(n * CHUNK, CHUNK), CHUNK)
        prod = (keyb[:, ts].astype(jnp.float32) * valb[:, ts].astype(jnp.float32)).astype(jnp.bfloat16)
        prod = prod.astype(jnp.float32).T
        for h in range(CH // LANES):
            xt[h, ts, :] = prod[:, h * LANES : (h + 1) * LANES]
        for h in range(CH // LANES):
            ls = slice(h * LANES, (h + 1) * LANES)
            a = [jnp.broadcast_to(coef[0, m : m + 1, ls], (8, LANES)) for m in range(MODES)]

            def step(i, hs):
                for u in range(4):
                    xv = xt[h, pl.ds(n * CHUNK + i * 4 + u, 8, stride=SUB), :]
                    hs = tuple(a[m] * hs[m] + xv for m in range(MODES))
                return hs

            hs = lax.fori_loop(0, SUB // 4, step, tuple(jnp.zeros((8, LANES), jnp.float32) for _ in range(MODES)))
            first = lax.broadcasted_iota(jnp.int32, (8, LANES), 0) == 0
            for m in range(MODES):
                s = hs[m]
                s = s + am1[m, :, ls] * pltpu.roll(s, 1, 0)
                s = s + am2[m, :, ls] * pltpu.roll(s, 2, 0)
                s = s + am4[m, :, ls] * pltpu.roll(s, 4, 0)
                est[n, m, :, ls] = jnp.where(first, 0.0, pltpu.roll(s, 1, 0))
                gtot[n, m : m + 1, ls] = s[7:8, :]
        return c0

    lax.fori_loop(0, NC, pass1, 0)

    final = jnp.zeros((MODES, CH), jnp.float32)
    for n in range(NC):
        final = coef[2] * final + gtot[n]
    fr[ctx] = final

    def state_copy(d, slot):
        return pltpu.make_async_remote_copy(
            fr.at[slot], fr.at[slot], fss.at[d], frs.at[d], device_id=peer(d), device_id_type=MESH
        )

    for d in range(1, CTX):
        state_copy(d, ctx).start()
    loads[2].wait()
    for d in range(1, CTX):
        state_copy(d, (ctx + CTX - d) % CTX).wait_recv()
    start = jnp.zeros((MODES, CH), jnp.float32)
    for j in range(CTX):
        gap = jnp.maximum(ctx - 1 - j, 0).astype(jnp.float32) * float(TOK)
        start = start + jnp.where(j < ctx, jnp.exp(-rate * gap) * fr[j], 0.0)
    carry[...] = start

    def conv(n):
        for h in range(CH // LANES):
            ls = slice(h * LANES, (h + 1) * LANES)
            a = [jnp.broadcast_to(coef[0, m : m + 1, ls], (8, LANES)) for m in range(MODES)]
            b = [jnp.broadcast_to(coef[1, m : m + 1, ls], (8, LANES)) for m in range(MODES)]
            skip = jnp.broadcast_to(skip_ref[:, ls], (8, LANES))

            def step(i, hs):
                for u in range(4):
                    at = pl.ds(n * CHUNK + i * 4 + u, 8, stride=SUB)
                    xv = xt[h, at, :]
                    hs = tuple(a[m] * hs[m] + xv for m in range(MODES))
                    terms = [skip * xv] + [b[m] * hs[m] for m in range(MODES)]
                    while len(terms) > 1:
                        terms = [
                            terms[q] + terms[q + 1] if q + 1 < len(terms) else terms[q]
                            for q in range(0, len(terms), 2)
                        ]
                    xt[h, at, :] = terms[0]
                return hs

            hs = tuple(
                est[n, m, :, ls] + apow[m, :, ls] * carry[m : m + 1, ls] for m in range(MODES)
            )
            lax.fori_loop(0, SUB // 4, step, hs)
        carry[...] = coef[2] * carry[...] + gtot[n]
        ts = pl.ds(pl.multiple_of(n * CHUNK, CHUNK), CHUNK)
        for h in range(CH // LANES):
            filtered = xt[h, ts, :].T
            rows = pl.ds(pl.multiple_of(me_slot * CH + h * LANES, LANES), LANES)
            gate = gateb[h * LANES : (h + 1) * LANES, ts].astype(jnp.float32)
            g[n, rows, :] = (gate * filtered).astype(jnp.bfloat16)

    def copy(kind, n, slot, device, half=None):
        first = slot * CH + (0 if half is None else half * (CH // 2))
        size = CH if half is None else CH // 2
        ref = g.at[n, pl.ds(pl.multiple_of(first, size), size), :]
        return pltpu.make_async_remote_copy(
            ref, ref, ss.at[kind, n], rs.at[kind, n], device_id=device, device_id_type=MESH
        )

    def y_copy(n):
        return pltpu.make_async_remote_copy(
            ysend.at[n], yrecv.at[n], ss.at[YY, n], rs.at[YY, n], device_id=y_dev, device_id_type=MESH
        )

    def out_copy(n):
        ts = pl.ds(pl.multiple_of(n * CHUNK, CHUNK), CHUNK)
        return pltpu.make_async_copy(ostage.at[n], out_hbm.at[:, ts], out_sem.at[n])

    s_prev, s_next, s_opp = slot_of(3, 0), slot_of(1, 0), slot_of(2, 0)
    o_me, o_prev, o_next, o_opp = slot_of(0, 1), slot_of(3, 1), slot_of(1, 1), slot_of(2, 1)

    def forward(n):
        copy(XP, n, s_prev, x_next).wait_recv()
        copy(F0, n, s_prev, x_next, 0).start()
        copy(CXM, n, s_prev, other).start()
        copy(XM, n, s_next, x_prev).wait_recv()
        copy(F1, n, s_next, x_prev, 1).start()
        copy(CXP, n, s_next, other).start()

    def opposite(n):
        copy(F0, n, s_opp, x_next, 0).wait_recv()
        copy(C0, n, s_opp, other, 0).start()
        copy(F1, n, s_opp, x_prev, 1).wait_recv()
        copy(C1, n, s_opp, other, 1).start()

    def weights():
        for c in own_w:
            c.wait()
        for dx, dc in plane:
            for yb in range(2):
                w_copy(dx, dc, yb, slot_of(NX - dx, dc)).wait_recv()
        for s in range(SLOTS):
            for yb in range(2):
                wt[yb * CH : (yb + 1) * CH, s * CH : (s + 1) * CH] = w[s, yb].T

    def project(n):
        copy(CO, n, o_me, other).wait_recv()
        copy(CXM, n, o_prev, other).wait_recv()
        copy(CXP, n, o_next, other).wait_recv()
        copy(C0, n, o_opp, other, 0).wait_recv()
        copy(C1, n, o_opp, other, 1).wait_recv()
        theirs = pl.ds(pl.multiple_of((1 - yh) * CH, CH), CH)
        mine = pl.ds(pl.multiple_of(yh * CH, CH), CH)
        ysend[n] = jnp.dot(wt[theirs, :], g[n], preferred_element_type=jnp.float32).astype(jnp.bfloat16)
        y_copy(n).start()
        pself[n] = jnp.dot(wt[mine, :], g[n], preferred_element_type=jnp.float32)

    def finish(n):
        y_copy(n).wait_recv()
        ostage[n] = (pself[n] + yrecv[n].astype(jnp.float32)).astype(jnp.bfloat16)
        out_copy(n).start()

    def turn(i, c0):
        @pl.when(i < NC)
        def _():
            conv(i)
            copy(XP, i, me_slot, x_next).start()
            copy(XM, i, me_slot, x_prev).start()
            copy(CO, i, me_slot, other).start()

        def at(lag, f):
            @pl.when(jnp.logical_and(i >= lag, i < NC + lag))
            def _():
                f(i - lag)

        at(LAG_FWD, forward)
        at(LAG_OPP, opposite)

        @pl.when(i == LAG_MM)
        def _():
            weights()

        at(LAG_MM, project)
        at(LAG_FIN, finish)
        return c0

    lax.fori_loop(0, NC + LAG_FIN, turn, 0)

    def drain(n, c0):
        copy(XP, n, me_slot, x_next).wait_send()
        copy(XM, n, me_slot, x_prev).wait_send()
        copy(CO, n, me_slot, other).wait_send()
        copy(F0, n, s_prev, x_next, 0).wait_send()
        copy(F1, n, s_next, x_prev, 1).wait_send()
        copy(CXM, n, s_prev, other).wait_send()
        copy(CXP, n, s_next, other).wait_send()
        copy(C0, n, s_opp, other, 0).wait_send()
        copy(C1, n, s_opp, other, 1).wait_send()
        y_copy(n).wait_send()
        out_copy(n).wait()
        return c0

    lax.fori_loop(0, NC, drain, 0)
    for dx, dc in plane:
        for yb in range(2):
            w_copy(dx, dc, yb, me_slot).wait_send()
    for d in range(1, CTX):
        state_copy(d, ctx).wait_send()


def on_device(key_feature, value_feature, query_gate, decay_rates, residues, skip_gain, out_weight):
    anywhere = pl.BlockSpec(memory_space=pl.ANY)
    local = pl.BlockSpec(memory_space=pltpu.VMEM)
    bf16, f32 = jnp.bfloat16, jnp.float32
    return pl.pallas_call(
        kernel,
        out_shape=jax.ShapeDtypeStruct((CH, TOK), bf16),
        in_specs=[anywhere, anywhere, anywhere, local, local, local, anywhere],
        out_specs=anywhere,
        scratch_shapes=[
            pltpu.VMEM((CH, TOK), bf16),
            pltpu.VMEM((CH, TOK), bf16),
            pltpu.VMEM((CH, TOK), bf16),
            pltpu.VMEM((CH // LANES, TOK, LANES), f32),
            pltpu.VMEM((NC, MODES, 8, CH), f32),
            pltpu.VMEM((NC, MODES, CH), f32),
            pltpu.VMEM((MODES, 8, CH), f32),
            pltpu.VMEM((MODES, 8, CH), f32),
            pltpu.VMEM((MODES, 8, CH), f32),
            pltpu.VMEM((MODES, 8, CH), f32),
            pltpu.VMEM((3, MODES, CH), f32),
            pltpu.VMEM((MODES, CH), f32),
            pltpu.VMEM((CTX, MODES, CH), f32),
            pltpu.VMEM((NC, SLOTS * CH, CHUNK), bf16),
            pltpu.VMEM((SLOTS, 2, CH, CH), bf16),
            pltpu.VMEM((2 * CH, SLOTS * CH), bf16),
            pltpu.VMEM((NC, CH, CHUNK), f32),
            pltpu.VMEM((NC, CH, CHUNK), bf16),
            pltpu.VMEM((NC, CH, CHUNK), bf16),
            pltpu.VMEM((NC, CH, CHUNK), bf16),
            pltpu.SemaphoreType.DMA((5,)),
            pltpu.SemaphoreType.DMA((NC,)),
            pltpu.SemaphoreType.DMA((10, NC)),
            pltpu.SemaphoreType.DMA((10, NC)),
            pltpu.SemaphoreType.DMA((CTX,)),
            pltpu.SemaphoreType.DMA((CTX,)),
            pltpu.SemaphoreType.DMA((SLOTS, 2)),
            pltpu.SemaphoreType.DMA((SLOTS, 2)),
        ],
        compiler_params=pltpu.CompilerParams(
            collective_id=0, has_side_effects=True, vmem_limit_bytes=56 * 2**20
        ),
        name="hyena",
    )(
        key_feature, value_feature, query_gate, decay_rates, residues,
        skip_gain.reshape(1, CH), out_weight,
    )


def solution(mesh):
    return jax.shard_map(
        on_device,
        mesh=mesh,
        in_specs=(
            P("tp", "ctx"), P("tp", "ctx"), P("tp", "ctx"),
            P(None, "tp"), P(None, "tp"), P("tp"), P("tp", None),
        ),
        out_specs=P("tp", "ctx"),
        check_vma=False,
    )
```

time: 358 us -> 84.3 us (0.24); the launches traced: 353 us -> 84.2 us
  waiting for transfers between devices: 149 us -> 0 us
  matrix products: 119 us -> 0 us
  Pallas kernels: 0 us -> 81.8 us
  other arithmetic: 26.4 us -> 0 us
  blocking collectives: 17.9 us -> 0 us
  between operations: 14.6 us -> 0.01 us
  starting transfers between devices: 12.1 us -> 0 us
  local copies, waits for them, and re-layouts: 14.3 us -> 2.3 us
    reduce_scatter x1 -> x0, waiting for transfers between devices: 149 us -> none  [on_device(): lax.psum_scatter(lax.dot_general(out_weight, gated, (((0,), (0,)), ((), (...]
    dot_general x15 -> x0, matrix products: 119 us -> none  [the longest x1 47.8 us: signal_spectrum(): jnp.einsum('ckn,nj->ckj', turned_re, inner_sin, precision=exact_mode)]
    pallas_call x0 -> x1, Pallas kernels: none -> 81.8 us  [on_device(): pl.pallas_call(kernel, out_shape=jax.ShapeDtypeStruct((CH, TOK), bf16), i...]
    all_to_all x1 -> x0, blocking collectives: 17.9 us -> none  [on_device(): lax.all_to_all(owned_gated, 'ctx', split_axis=1, concat_axis=0, tiled=True)]
    all_to_all x2 -> x0, starting transfers between devices: 12 us -> none  [the longest x1 6.88 us: on_device(): lax.all_to_all(product, 'ctx', split_axis=0, concat_axis=1, tiled=True)]
    sub x1 -> x0, other arithmetic: 6.26 us -> none  [convolve(): joint_re = signal_re * taps_re - signal_im * taps_im]
    convert_element_type x2 -> x0, other arithmetic: 6.24 us -> none  [the longest x1 3.18 us: on_device(): (owned_gate.astype(jnp.float32) * filtered).astype(jnp.bfloat16)]
    mul x9 -> x0, other arithmetic: 5.5 us -> none  [the longest x8 5.5 us: taps_spectrum(): 4.0 * ratio * half_sq[None]]
  transfers between devices with their start and end apart: 3 -> 0, of which waited for: 1 -> 0; matrix products, arithmetic and copies ran while one was open for 40% -> 0% of each run, Pallas kernels for 0% -> 0%
where the time goes in v1:
time: 84.3 us; the launch traced here: 84.2 us
  Pallas kernels  81.8 us (97%)
  local copies, waits for them, and re-layouts  2.3 us (3%)
    pallas_call x1, Pallas kernels, on_device(): pl.pallas_call(kernel, out_shape=jax.ShapeDtypeStruct((CH, TOK), bf16), i...  81.8 us
    unnamed x1, local copies, waits for them, and re-layouts  2.3 us

profile of v1, /device:TPU:1, one launch (start us, length us, event | category | flops | bytes accessed | tf_op | source)
XLA Modules:
  0.0 84.2 jit_solution(12043254993991513961)
XLA Ops:
  0.0 81.8 %hyena.1 = bf16[256,2048]{1,0:T(8,128)(2,1)} custom-call(bf16[256,2048]{1,0:T(8,128)(2,1)} %key_hbm.1, bf16[256,2048]{1,0:T(8,128)(2,1)} %val_hbm.1, bf16[256,2048]{1,0:T(8,128)(2,1)} %gate_hbm.1, f32[16,256]{1,0:T(8,128)} %rate_ref.1, f32[16,256]{1,0:T(8,128)} %res_ref.1, f32[1,256]{1,0:T(1,128)} %bitcast.1, bf16[256,4096]{1,0:T(8,128)(2,1)} %w_hbm.1), custom_call_target="tpu_custom_call" | custom-call | tf_op jit(solution)/shard_map/hyena/pallas_call | solution.py:303
  81.8 2.3 %copy.9 = bf16[256,2048]{1,0:T(8,128)(2,1)} copy(bf16[256,2048]{1,0:T(8,128)(2,1)} %hyena.1) | data formatting | bytes 2097152

commit v2 on v1

v2 whole, which is shorter than its diff:
```python
import functools

import jax
import jax.numpy as jnp
from jax import lax
from jax.experimental import pallas as pl
from jax.experimental.pallas import tpu as pltpu
from jax.sharding import PartitionSpec as P

MESH = pl.DeviceIdType.MESH

MODES = 16
CH = 256
TOK = 2048
CHUNK = 256
NC = TOK // CHUNK
NU = NC + 1
SUB = 32
PITCH = 40
LANES = 128
CTX = 8
NX = 4
SLOTS = 8
W_DIRECT = 64
W_PART = (CH - W_DIRECT) // 4

XP, XM, CO, F0, F1, CXM, CXP, C0, C1, YY = range(10)
LAG_FWD, LAG_OPP, LAG_MM, LAG_FIN = 1, 2, 4, 6


def kernel(
    key_hbm, val_hbm, gate_hbm, rate_ref, res_ref, skip_ref, w_hbm, out_ref,
    keyb, valb, gateb, xt, est, gtot, am1, am2, am4, apow, coef, carry, fr,
    g, w, pself, ysend, yrecv,
    in_sem, ss, rs, fss, frs, wss, wrs, zss, zrs,
):
    ctx = lax.axis_index("ctx")
    tp = lax.axis_index("tp")
    x = tp // 4
    yh = (tp // 2) % 2
    core = tp % 2

    def dev(dx, dy, dc):
        return (ctx, ((x + dx) % NX) * 4 + ((yh + dy) % 2) * 2 + (core + dc) % 2)

    def peer(d):
        return ((ctx + d) % CTX, tp)

    x_next, x_prev, other, y_dev = dev(1, 0, 0), dev(3, 0, 0), dev(0, 0, 1), dev(0, 1, 0)
    plane = [(dx, dc) for dx in range(NX) for dc in range(2) if (dx, dc) != (0, 0)]

    barrier = pltpu.get_barrier_semaphore()
    for dx, dc in plane:
        pl.semaphore_signal(barrier, inc=1, device_id=dev(dx, 0, dc), device_id_type=MESH)
    pl.semaphore_signal(barrier, inc=1, device_id=y_dev, device_id_type=MESH)
    for d in range(1, CTX):
        pl.semaphore_signal(barrier, inc=1, device_id=peer(d), device_id_type=MESH)

    loads = [
        pltpu.make_async_copy(key_hbm, keyb, in_sem.at[0]),
        pltpu.make_async_copy(val_hbm, valb, in_sem.at[1]),
        pltpu.make_async_copy(gate_hbm, gateb, in_sem.at[2]),
    ]
    for c in loads:
        c.start()

    def slot_of(dx, dc):
        return ((x + dx) % NX) * 2 + (core + dc) % 2

    me_slot = slot_of(0, 0)

    z = ctx % 4

    def z_rows(d):
        return pl.ds(pl.multiple_of(W_DIRECT + ((z + d) % 4) * W_PART, 16), W_PART)

    w_rows = (z_rows(0), pl.ds(0, W_DIRECT))

    def w_cols(dx, dc, yb, part):
        col = (((x + dx) % NX) * 4 + yb * 2 + (core + dc) % 2) * CH
        return w_hbm.at[w_rows[part], pl.ds(pl.multiple_of(col, CH), CH)]

    own_w = [
        pltpu.make_async_copy(
            w_cols(0, 0, yb, part), w.at[me_slot, yb, w_rows[part]], in_sem.at[3 + part * 2 + yb]
        )
        for part in range(2)
        for yb in range(2)
    ]
    for c in own_w:
        c.start()

    def w_copy(dx, dc, yb, part, slot):
        i = dx * 2 + dc
        return pltpu.make_async_remote_copy(
            w_cols(dx, dc, yb, part), w.at[slot, yb, w_rows[part]], wss.at[i, yb, part], wrs.at[i, yb, part],
            device_id=dev(dx, 0, dc), device_id_type=MESH,
        )

    def z_copy(d, rows):
        part = w.at[:, :, rows, :]
        return pltpu.make_async_remote_copy(
            part, part, zss.at[d], zrs.at[d],
            device_id=((ctx // 4) * 4 + (z + d) % 4, tp), device_id_type=MESH,
        )

    rate = rate_ref[...]
    for m in range(MODES):
        r8 = jnp.broadcast_to(rate[m : m + 1, :], (8, CH))
        sub = lax.broadcasted_iota(jnp.int32, (8, CH), 0)
        subf = sub.astype(jnp.float32)
        am1[m] = jnp.where(sub >= 1, jnp.exp(-r8 * float(SUB)), 0.0)
        am2[m] = jnp.where(sub >= 2, jnp.exp(-r8 * float(2 * SUB)), 0.0)
        am4[m] = jnp.where(sub >= 4, jnp.exp(-r8 * float(4 * SUB)), 0.0)
        apow[m] = jnp.exp(-r8 * (subf * float(SUB)))
    coef[0] = jnp.exp(-rate)
    coef[1] = res_ref[...] * jnp.sqrt(2.0 * rate / MODES)
    coef[2] = jnp.exp(-rate * float(CHUNK))

    pl.semaphore_wait(barrier, len(plane) + 1 + CTX - 1)
    for part in range(2):
        for dx, dc in plane:
            for yb in range(2):
                w_copy(dx, dc, yb, part, me_slot).start()

    loads[0].wait()
    loads[1].wait()

    def sub_rows(n, q):
        return pl.ds(pl.multiple_of((n * 8 + q) * PITCH, 8), SUB)

    def step_rows(n, i):
        return pl.ds(n * (8 * PITCH) + i, 8, stride=PITCH)

    def pass1(n, c0):
        ts = pl.ds(pl.multiple_of(n * CHUNK, CHUNK), CHUNK)
        prod = (keyb[:, ts].astype(jnp.float32) * valb[:, ts].astype(jnp.float32)).astype(jnp.bfloat16)
        prod = prod.astype(jnp.float32).T
        for h in range(CH // LANES):
            for q in range(8):
                xt[h, sub_rows(n, q), :] = prod[q * SUB : (q + 1) * SUB, h * LANES : (h + 1) * LANES]
        for h in range(CH // LANES):
            ls = slice(h * LANES, (h + 1) * LANES)
            a = [jnp.broadcast_to(coef[0, m : m + 1, ls], (8, LANES)) for m in range(MODES)]

            hs = [jnp.zeros((8, LANES), jnp.float32)] * MODES
            for i in range(SUB):
                xv = xt[h, step_rows(n, i), :]
                hs = [a[m] * hs[m] + xv for m in range(MODES)]
            first = lax.broadcasted_iota(jnp.int32, (8, LANES), 0) == 0
            for m in range(MODES):
                s = hs[m]
                s = s + am1[m, :, ls] * pltpu.roll(s, 1, 0)
                s = s + am2[m, :, ls] * pltpu.roll(s, 2, 0)
                s = s + am4[m, :, ls] * pltpu.roll(s, 4, 0)
                est[n, m, :, ls] = jnp.where(first, 0.0, pltpu.roll(s, 1, 0))
                gtot[n, m : m + 1, ls] = s[7:8, :]
        return c0

    lax.fori_loop(0, NC, pass1, 0)

    final = jnp.zeros((MODES, CH), jnp.float32)
    for n in range(NC):
        final = coef[2] * final + gtot[n]
    fr[ctx] = final

    def state_copy(d, slot):
        return pltpu.make_async_remote_copy(
            fr.at[slot], fr.at[slot], fss.at[d], frs.at[d], device_id=peer(d), device_id_type=MESH
        )

    for d in range(1, CTX):
        state_copy(d, ctx).start()
    loads[2].wait()

    for c in own_w[:2]:
        c.wait()
    for dx, dc in plane:
        for yb in range(2):
            w_copy(dx, dc, yb, 0, slot_of(NX - dx, dc)).wait_recv()
    for d in range(1, 4):
        z_copy(d, z_rows(0)).start()

    for d in range(1, CTX):
        state_copy(d, (ctx + CTX - d) % CTX).wait_recv()
    start = jnp.zeros((MODES, CH), jnp.float32)
    for j in range(CTX):
        gap = jnp.maximum(ctx - 1 - j, 0).astype(jnp.float32) * float(TOK)
        start = start + jnp.where(j < ctx, jnp.exp(-rate * gap) * fr[j], 0.0)
    carry[...] = start

    def conv(n):
        for h in range(CH // LANES):
            ls = slice(h * LANES, (h + 1) * LANES)
            a = [jnp.broadcast_to(coef[0, m : m + 1, ls], (8, LANES)) for m in range(MODES)]
            b = [jnp.broadcast_to(coef[1, m : m + 1, ls], (8, LANES)) for m in range(MODES)]
            skip = jnp.broadcast_to(skip_ref[:, ls], (8, LANES))

            hs = [est[n, m, :, ls] + apow[m, :, ls] * carry[m : m + 1, ls] for m in range(MODES)]
            for i in range(SUB):
                at = step_rows(n, i)
                xv = xt[h, at, :]
                hs = [a[m] * hs[m] + xv for m in range(MODES)]
                terms = [skip * xv] + [b[m] * hs[m] for m in range(MODES)]
                while len(terms) > 1:
                    terms = [
                        terms[q] + terms[q + 1] if q + 1 < len(terms) else terms[q]
                        for q in range(0, len(terms), 2)
                    ]
                xt[h, at, :] = terms[0]
        carry[...] = coef[2] * carry[...] + gtot[n]
        ts = pl.ds(pl.multiple_of(n * CHUNK, CHUNK), CHUNK)
        for h in range(CH // LANES):
            filtered = jnp.concatenate([xt[h, sub_rows(n, q), :] for q in range(8)], axis=0).T
            rows = pl.ds(pl.multiple_of(me_slot * CH + h * LANES, LANES), LANES)
            gate = gateb[h * LANES : (h + 1) * LANES, ts].astype(jnp.float32)
            g[n, rows, :] = (gate * filtered).astype(jnp.bfloat16)

    def lanes_of(u, full):
        if full:
            return u, pl.ds(0, CHUNK)
        return NC - 1, pl.ds(pl.multiple_of((u - (NC - 1)) * LANES, LANES), LANES)

    def copy(kind, u, full, slot, device, half=None):
        n, lanes = lanes_of(u, full)
        first = slot * CH + (0 if half is None else half * (CH // 2))
        size = CH if half is None else CH // 2
        ref = g.at[n, pl.ds(pl.multiple_of(first, size), size), lanes]
        return pltpu.make_async_remote_copy(
            ref, ref, ss.at[kind, u], rs.at[kind, u], device_id=device, device_id_type=MESH
        )

    def y_copy(u, full):
        n, lanes = lanes_of(u, full)
        return pltpu.make_async_remote_copy(
            ysend.at[n, :, lanes], yrecv.at[n, :, lanes], ss.at[YY, u], rs.at[YY, u],
            device_id=y_dev, device_id_type=MESH,
        )

    s_prev, s_next, s_opp = slot_of(3, 0), slot_of(1, 0), slot_of(2, 0)
    o_me, o_prev, o_next, o_opp = slot_of(0, 1), slot_of(3, 1), slot_of(1, 1), slot_of(2, 1)

    def send(u, full):
        copy(XP, u, full, me_slot, x_next).start()
        copy(XM, u, full, me_slot, x_prev).start()
        copy(CO, u, full, me_slot, other).start()

    def forward(u, full):
        copy(XP, u, full, s_prev, x_next).wait_recv()
        copy(F0, u, full, s_prev, x_next, 0).start()
        copy(CXM, u, full, s_prev, other).start()
        copy(XM, u, full, s_next, x_prev).wait_recv()
        copy(F1, u, full, s_next, x_prev, 1).start()
        copy(CXP, u, full, s_next, other).start()

    def opposite(u, full):
        copy(F0, u, full, s_opp, x_next, 0).wait_recv()
        copy(C0, u, full, s_opp, other, 0).start()
        copy(F1, u, full, s_opp, x_prev, 1).wait_recv()
        copy(C1, u, full, s_opp, other, 1).start()

    def weights():
        for c in own_w[2:]:
            c.wait()
        for dx, dc in plane:
            for yb in range(2):
                w_copy(dx, dc, yb, 1, slot_of(NX - dx, dc)).wait_recv()
        for d in range(1, 4):
            z_copy(d, z_rows(4 - d)).wait_recv()

    def project(u, full):
        copy(CO, u, full, o_me, other).wait_recv()
        copy(CXM, u, full, o_prev, other).wait_recv()
        copy(CXP, u, full, o_next, other).wait_recv()
        copy(C0, u, full, o_opp, other, 0).wait_recv()
        copy(C1, u, full, o_opp, other, 1).wait_recv()
        n, lanes = lanes_of(u, full)

        def partial(yb):
            total = None
            for slot in range(SLOTS):
                term = lax.dot_general(
                    w[slot, yb], g[n, slot * CH : (slot + 1) * CH, lanes],
                    (((0,), (0,)), ((), ())), preferred_element_type=jnp.float32,
                )
                total = term if total is None else total + term
            return total

        ysend[n, :, lanes] = partial(1 - yh).astype(jnp.bfloat16)
        y_copy(u, full).start()
        pself[n, :, lanes] = partial(yh)

    def finish(u, full):
        y_copy(u, full).wait_recv()
        n, lanes = lanes_of(u, full)
        if full:
            ts = pl.ds(pl.multiple_of(n * CHUNK, CHUNK), CHUNK)
        else:
            ts = pl.ds(pl.multiple_of(u * LANES + (NC - 1) * LANES, LANES), LANES)
        out_ref[:, ts] = (pself[n, :, lanes] + yrecv[n, :, lanes].astype(jnp.float32)).astype(jnp.bfloat16)

    def turn(i, c0):
        @pl.when(i < NC)
        def _():
            conv(i)

        def at(lag, f):
            u = i - lag

            @pl.when(jnp.logical_and(u >= 0, u < NC - 1))
            def _():
                f(u, True)

            @pl.when(jnp.logical_and(u >= NC - 1, u < NU))
            def _():
                f(u, False)

        at(0, send)
        at(LAG_FWD, forward)
        at(LAG_OPP, opposite)

        @pl.when(i == LAG_MM)
        def _():
            weights()

        at(LAG_MM, project)
        at(LAG_FIN, finish)
        return c0

    lax.fori_loop(0, NU + LAG_FIN, turn, 0)

    def drain(full):
        def body(u, c0):
            copy(XP, u, full, me_slot, x_next).wait_send()
            copy(XM, u, full, me_slot, x_prev).wait_send()
            copy(CO, u, full, me_slot, other).wait_send()
            copy(F0, u, full, s_prev, x_next, 0).wait_send()
            copy(F1, u, full, s_next, x_prev, 1).wait_send()
            copy(CXM, u, full, s_prev, other).wait_send()
            copy(CXP, u, full, s_next, other).wait_send()
            copy(C0, u, full, s_opp, other, 0).wait_send()
            copy(C1, u, full, s_opp, other, 1).wait_send()
            y_copy(u, full).wait_send()
            return c0

        return body

    lax.fori_loop(0, NC - 1, drain(True), 0)
    lax.fori_loop(NC - 1, NU, drain(False), 0)
    for dx, dc in plane:
        for yb in range(2):
            for part in range(2):
                w_copy(dx, dc, yb, part, me_slot).wait_send()
    for d in range(1, 4):
        z_copy(d, z_rows(0)).wait_send()
    for d in range(1, CTX):
        state_copy(d, ctx).wait_send()


def on_device(key_feature, value_feature, query_gate, decay_rates, residues, skip_gain, out_weight):
    anywhere = pl.BlockSpec(memory_space=pl.ANY)
    local = pl.BlockSpec(memory_space=pltpu.VMEM)
    bf16, f32 = jnp.bfloat16, jnp.float32
    return pl.pallas_call(
        kernel,
        out_shape=pltpu.VMEM((CH, TOK), bf16),
        in_specs=[anywhere, anywhere, anywhere, local, local, local, anywhere],
        out_specs=local,
        scratch_shapes=[
            pltpu.VMEM((CH, TOK), bf16),
            pltpu.VMEM((CH, TOK), bf16),
            pltpu.VMEM((CH, TOK), bf16),
            pltpu.VMEM((CH // LANES, TOK // SUB * PITCH, LANES), f32),
            pltpu.VMEM((NC, MODES, 8, CH), f32),
            pltpu.VMEM((NC, MODES, CH), f32),
            pltpu.VMEM((MODES, 8, CH), f32),
            pltpu.VMEM((MODES, 8, CH), f32),
            pltpu.VMEM((MODES, 8, CH), f32),
            pltpu.VMEM((MODES, 8, CH), f32),
            pltpu.VMEM((3, MODES, CH), f32),
            pltpu.VMEM((MODES, CH), f32),
            pltpu.VMEM((CTX, MODES, CH), f32),
            pltpu.VMEM((NC, SLOTS * CH, CHUNK), bf16),
            pltpu.VMEM((SLOTS, 2, CH, CH), bf16),
            pltpu.VMEM((NC, CH, CHUNK), f32),
            pltpu.VMEM((NC, CH, CHUNK), bf16),
            pltpu.VMEM((NC, CH, CHUNK), bf16),
            pltpu.SemaphoreType.DMA((7,)),
            pltpu.SemaphoreType.DMA((10, NU)),
            pltpu.SemaphoreType.DMA((10, NU)),
            pltpu.SemaphoreType.DMA((CTX,)),
            pltpu.SemaphoreType.DMA((CTX,)),
            pltpu.SemaphoreType.DMA((SLOTS, 2, 2)),
            pltpu.SemaphoreType.DMA((SLOTS, 2, 2)),
            pltpu.SemaphoreType.DMA((4,)),
            pltpu.SemaphoreType.DMA((4,)),
        ],
        compiler_params=pltpu.CompilerParams(
            collective_id=0, has_side_effects=True, vmem_limit_bytes=56 * 2**20
        ),
        name="hyena",
    )(
        key_feature, value_feature, query_gate, decay_rates, residues,
        skip_gain.reshape(1, CH), out_weight,
    )


def solution(mesh):
    return jax.shard_map(
        on_device,
        mesh=mesh,
        in_specs=(
            P("tp", "ctx"), P("tp", "ctx"), P("tp", "ctx"),
            P(None, "tp"), P(None, "tp"), P("tp"), P("tp", None),
        ),
        out_specs=P("tp", "ctx"),
        check_vma=False,
    )
```

time: 84.3 us -> 70 us (0.83)
  Pallas kernels: 81.8 us -> 68.4 us
  local copies, waits for them, and re-layouts: 2.3 us -> 0.97 us
    pallas_call x1, Pallas kernels: 81.8 us -> 68.4 us  [on_device(): pl.pallas_call(kernel, out_shape=pltpu.VMEM((CH, TOK), bf16), in_specs=[a...]
    unnamed x1, local copies, waits for them, and re-layouts: 2.3 us -> 0.97 us
where the time goes in v2:
time: 70 us; the launch traced here: 69.4 us
  Pallas kernels  68.4 us (98%)
  local copies, waits for them, and re-layouts  0.97 us (1%)
    pallas_call x1, Pallas kernels, on_device(): pl.pallas_call(kernel, out_shape=pltpu.VMEM((CH, TOK), bf16), in_specs=[a...  68.4 us

profile of v2, /device:TPU:1, one launch (start us, length us, event | category | flops | bytes accessed | tf_op | source)
XLA Modules:
  0.0 69.4 jit_solution(16635692821327844826)
XLA Ops:
  0.0 68.4 %hyena.1 = bf16[256,2048]{1,0:T(8,128)(2,1)S(1)} custom-call(bf16[256,2048]{1,0:T(8,128)(2,1)} %key_hbm.1, bf16[256,2048]{1,0:T(8,128)(2,1)} %val_hbm.1, bf16[256,2048]{1,0:T(8,128)(2,1)} %gate_hbm.1, f32[16,256]{1,0:T(8,128)} %rate_ref.1, f32[16,256]{1,0:T(8,128)} %res_ref.1, f32[1,256]{1,0:T(1,128)} %bitcast.1, bf16[256,4096]{1,0:T(8,128)(2,1)} %w_hbm.1), custom_call_target="tpu_custom_call" | custom-call | tf_op jit(solution)/shard_map/hyena/pallas_call | solution.py:364
  68.4 1.0 %copy.9 = bf16[256,2048]{1,0:T(8,128)(2,1)} copy(bf16[256,2048]{1,0:T(8,128)(2,1)S(1)} %hyena.1) | data formatting | bytes 2097152

commit v3 on v2

--- a/solution.py
+++ b/solution.py
@@ -21,18 +21,18 @@
 CTX = 8
 NX = 4
 SLOTS = 8
-W_DIRECT = 64
-W_PART = (CH - W_DIRECT) // 4
+W_Z = 128
 
 XP, XM, CO, F0, F1, CXM, CXP, C0, C1, YY = range(10)
-LAG_FWD, LAG_OPP, LAG_MM, LAG_FIN = 1, 2, 4, 6
+TURNS = NU + 4
+EARLY = 0
 
 
 def kernel(
     key_hbm, val_hbm, gate_hbm, rate_ref, res_ref, skip_ref, w_hbm, out_ref,
     keyb, valb, gateb, xt, est, gtot, am1, am2, am4, apow, coef, carry, fr,
     g, w, pself, ysend, yrecv,
-    in_sem, ss, rs, fss, frs, wss, wrs, zss, zrs,
+    in_sem, ss, rs, fss, frs, wss, wrs, zss, zrs, ready_sem,
 ):
     ctx = lax.axis_index("ctx")
     tp = lax.axis_index("tp")
@@ -43,8 +43,13 @@
     def dev(dx, dy, dc):
         return (ctx, ((x + dx) % NX) * 4 + ((yh + dy) % 2) * 2 + (core + dc) % 2)
 
-    def peer(d):
-        return ((ctx + d) % CTX, tp)
+    z = ctx % 4
+    y_lo = ctx // 4
+
+    def peer(dy, dz):
+        return (((y_lo + dy) % 2) * 4 + (z + dz) % 4, tp)
+
+    along = [(dy, dz) for dy in range(2) for dz in range(4) if (dy, dz) != (0, 0)]
 
     x_next, x_prev, other, y_dev = dev(1, 0, 0), dev(3, 0, 0), dev(0, 0, 1), dev(0, 1, 0)
     plane = [(dx, dc) for dx in range(NX) for dc in range(2) if (dx, dc) != (0, 0)]
@@ -53,8 +58,13 @@
     for dx, dc in plane:
         pl.semaphore_signal(barrier, inc=1, device_id=dev(dx, 0, dc), device_id_type=MESH)
     pl.semaphore_signal(barrier, inc=1, device_id=y_dev, device_id_type=MESH)
-    for d in range(1, CTX):
-        pl.semaphore_signal(barrier, inc=1, device_id=peer(d), device_id_type=MESH)
+    pl.semaphore_signal(barrier, inc=1, device_id=peer(1, 0), device_id_type=MESH)
+    for dy in range(2):
+        for dz in range(1, 4):
+
+            @pl.when(z + dz < 4)
+            def _():
+                pl.semaphore_signal(barrier, inc=1, device_id=peer(dy, dz), device_id_type=MESH)
 
     loads = [
         pltpu.make_async_copy(key_hbm, keyb, in_sem.at[0]),
@@ -69,12 +79,14 @@
 
     me_slot = slot_of(0, 0)
 
-    z = ctx % 4
-
     def z_rows(d):
-        return pl.ds(pl.multiple_of(W_DIRECT + ((z + d) % 4) * W_PART, 16), W_PART)
-
-    w_rows = (z_rows(0), pl.ds(0, W_DIRECT))
+        return pl.ds(pl.multiple_of(((z + d) % 4) * (W_Z // 4), 16), W_Z // 4)
+
+    def y_rows(d):
+        half = (CH - W_Z) // 2
+        return pl.ds(pl.multiple_of(W_Z + ((y_lo + d) % 2) * half, 16), half)
+
+    w_rows = (z_rows(0), y_rows(0))
 
     def w_cols(dx, dc, yb, part):
         col = (((x + dx) % NX) * 4 + yb * 2 + (core + dc) % 2) * CH
@@ -97,11 +109,10 @@
             device_id=dev(dx, 0, dc), device_id_type=MESH,
         )
 
-    def z_copy(d, rows):
+    def share_copy(d, rows):
         part = w.at[:, :, rows, :]
         return pltpu.make_async_remote_copy(
-            part, part, zss.at[d], zrs.at[d],
-            device_id=((ctx // 4) * 4 + (z + d) % 4, tp), device_id_type=MESH,
+            part, part, zss.at[d], zrs.at[d], device_id=peer(d // 4, d % 4), device_id_type=MESH
         )
 
     rate = rate_ref[...]
@@ -116,12 +127,6 @@
     coef[0] = jnp.exp(-rate)
     coef[1] = res_ref[...] * jnp.sqrt(2.0 * rate / MODES)
     coef[2] = jnp.exp(-rate * float(CHUNK))
-
-    pl.semaphore_wait(barrier, len(plane) + 1 + CTX - 1)
-    for part in range(2):
-        for dx, dc in plane:
-            for yb in range(2):
-                w_copy(dx, dc, yb, part, me_slot).start()
 
     loads[0].wait()
     loads[1].wait()
@@ -157,37 +162,82 @@
                 gtot[n, m : m + 1, ls] = s[7:8, :]
         return c0
 
-    lax.fori_loop(0, NC, pass1, 0)
+    lax.fori_loop(0, EARLY, pass1, 0)
+    pl.semaphore_wait(barrier, len(plane) + 2 + 2 * z)
+    for dy in range(2):
+        for dz in range(1, 4):
+
+            @pl.when(z >= dz)
+            def _():
+                pl.semaphore_signal(
+                    ready_sem.at[dz], inc=1, device_id=peer(dy, 4 - dz), device_id_type=MESH
+                )
+
+    for part in range(2):
+        for dx, dc in plane:
+            for yb in range(2):
+                w_copy(dx, dc, yb, part, me_slot).start()
+
+    lax.fori_loop(EARLY, NC, pass1, 0)
 
     final = jnp.zeros((MODES, CH), jnp.float32)
     for n in range(NC):
         final = coef[2] * final + gtot[n]
     fr[ctx] = final
 
-    def state_copy(d, slot):
+    def state_copy(dy, dz, slot):
+        i = dy * 4 + dz
         return pltpu.make_async_remote_copy(
-            fr.at[slot], fr.at[slot], fss.at[d], frs.at[d], device_id=peer(d), device_id_type=MESH
-        )
-
-    for d in range(1, CTX):
-        state_copy(d, ctx).start()
+            fr.at[slot], fr.at[slot], fss.at[i], frs.at[i], device_id=peer(dy, dz), device_id_type=MESH
+        )
+
+    def goes(dy, dz):
+        up = z + dz < 4
+        return (up if dz else False) if dy == 0 else y_lo == 0
+
+    def higher(dz):
+        @pl.when(z + dz < 4)
+        def _():
+            pl.semaphore_wait(ready_sem.at[dz], 2)
+            state_copy(0, dz, ctx).start()
+
+            @pl.when(y_lo == 0)
+            def _():
+                state_copy(1, dz, ctx).start()
+
+    for dz in range(4):
+
+        @pl.when(jnp.logical_and(y_lo == 0, jnp.logical_or(dz == 0, z + dz >= 4)))
+        def _():
+            state_copy(1, dz, ctx).start()
+
+    for dz in range(1, 4):
+        higher(dz)
+
+    def share(part):
+        for c in own_w[2 * part : 2 * part + 2]:
+            c.wait()
+        for dx, dc in plane:
+            for yb in range(2):
+                w_copy(dx, dc, yb, part, slot_of(NX - dx, dc)).wait_recv()
+        if part == 0:
+            for d in range(1, 4):
+                share_copy(d, z_rows(0)).start()
+        else:
+            share_copy(4, y_rows(0)).start()
+
+    share(0)
     loads[2].wait()
-
-    for c in own_w[:2]:
-        c.wait()
-    for dx, dc in plane:
-        for yb in range(2):
-            w_copy(dx, dc, yb, 0, slot_of(NX - dx, dc)).wait_recv()
-    for d in range(1, 4):
-        z_copy(d, z_rows(0)).start()
-
-    for d in range(1, CTX):
-        state_copy(d, (ctx + CTX - d) % CTX).wait_recv()
-    start = jnp.zeros((MODES, CH), jnp.float32)
-    for j in range(CTX):
-        gap = jnp.maximum(ctx - 1 - j, 0).astype(jnp.float32) * float(TOK)
-        start = start + jnp.where(j < ctx, jnp.exp(-rate * gap) * fr[j], 0.0)
-    carry[...] = start
+    carry[...] = jnp.zeros((MODES, CH), jnp.float32)
+    for dy, dz in along:
+
+        @pl.when(z >= dz if dy == 0 else y_lo == 1)
+        def _():
+            slot = ((y_lo + dy) % 2) * 4 + (z + 4 - dz) % 4
+            state_copy(dy, dz, slot).wait_recv()
+            gap = dz - 1 if dy == 0 else jnp.where(z >= dz, dz + 3, dz - 1)
+            gap = jnp.asarray(gap, jnp.int32).astype(jnp.float32) * float(TOK)
+            carry[...] += jnp.exp(-rate_ref[...] * gap) * fr[slot]
 
     def conv(n):
         for h in range(CH // LANES):
@@ -260,13 +310,9 @@
         copy(C1, u, full, s_opp, other, 1).start()
 
     def weights():
-        for c in own_w[2:]:
-            c.wait()
-        for dx, dc in plane:
-            for yb in range(2):
-                w_copy(dx, dc, yb, 1, slot_of(NX - dx, dc)).wait_recv()
         for d in range(1, 4):
-            z_copy(d, z_rows(4 - d)).wait_recv()
+            share_copy(d, z_rows(4 - d)).wait_recv()
+        share_copy(4, y_rows(1)).wait_recv()
 
     def project(u, full):
         copy(CO, u, full, o_me, other).wait_recv()
@@ -299,62 +345,80 @@
             ts = pl.ds(pl.multiple_of(u * LANES + (NC - 1) * LANES, LANES), LANES)
         out_ref[:, ts] = (pself[n, :, lanes] + yrecv[n, :, lanes].astype(jnp.float32)).astype(jnp.bfloat16)
 
+    def drain(u, full):
+        copy(XP, u, full, me_slot, x_next).wait_send()
+        copy(XM, u, full, me_slot, x_prev).wait_send()
+        copy(CO, u, full, me_slot, other).wait_send()
+        copy(F0, u, full, s_prev, x_next, 0).wait_send()
+        copy(F1, u, full, s_next, x_prev, 1).wait_send()
+        copy(CXM, u, full, s_prev, other).wait_send()
+        copy(CXP, u, full, s_next, other).wait_send()
+        copy(C0, u, full, s_opp, other, 0).wait_send()
+        copy(C1, u, full, s_opp, other, 1).wait_send()
+        y_copy(u, full).wait_send()
+
+    def drain_start():
+        for dx, dc in plane:
+            for yb in range(2):
+                for part in range(2):
+                    w_copy(dx, dc, yb, part, me_slot).wait_send()
+        for d in range(1, 4):
+            share_copy(d, z_rows(0)).wait_send()
+        share_copy(4, y_rows(0)).wait_send()
+        for dy, dz in along:
+
+            @pl.when(goes(dy, dz))
+            def _():
+                state_copy(dy, dz, ctx).wait_send()
+
     def turn(i, c0):
         @pl.when(i < NC)
         def _():
             conv(i)
 
-        def at(lag, f):
+        def at(lag, f, first=0, end=NU):
             u = i - lag
-
-            @pl.when(jnp.logical_and(u >= 0, u < NC - 1))
-            def _():
-                f(u, True)
-
-            @pl.when(jnp.logical_and(u >= NC - 1, u < NU))
-            def _():
-                f(u, False)
+            for lo, hi, full in ((first, min(end, NC - 1), True), (max(first, NC - 1), end, False)):
+                if lo < hi:
+
+                    @pl.when(jnp.logical_and(u >= lo, u < hi))
+                    def _():
+                        f(u, full)
 
         at(0, send)
-        at(LAG_FWD, forward)
-        at(LAG_OPP, opposite)
-
-        @pl.when(i == LAG_MM)
+        at(1, forward)
+        at(2, opposite)
+
+        @pl.when(i == 1)
+        def _():
+            share(1)
+
+        @pl.when(i == 4)
         def _():
             weights()
 
-        at(LAG_MM, project)
-        at(LAG_FIN, finish)
+        at(4, project, 0, 2)
+        at(3, project, 2, NU)
+        at(6, finish, 0, 2)
+        at(5, finish, 2, NC - 1)
+        at(4, finish, NC - 1, NU)
+        at(7, drain, 0, TURNS - 7)
+
+        @pl.when(i == 6)
+        def _():
+            drain_start()
+
         return c0
 
-    lax.fori_loop(0, NU + LAG_FIN, turn, 0)
-
-    def drain(full):
-        def body(u, c0):
-            copy(XP, u, full, me_slot, x_next).wait_send()
-            copy(XM, u, full, me_slot, x_prev).wait_send()
-            copy(CO, u, full, me_slot, other).wait_send()
-            copy(F0, u, full, s_prev, x_next, 0).wait_send()
-            copy(F1, u, full, s_next, x_prev, 1).wait_send()
-            copy(CXM, u, full, s_prev, other).wait_send()
-            copy(CXP, u, full, s_next, other).wait_send()
-            copy(C0, u, full, s_opp, other, 0).wait_send()
-            copy(C1, u, full, s_opp, other, 1).wait_send()
-            y_copy(u, full).wait_send()
-            return c0
-
-        return body
-
-    lax.fori_loop(0, NC - 1, drain(True), 0)
-    lax.fori_loop(NC - 1, NU, drain(False), 0)
-    for dx, dc in plane:
-        for yb in range(2):
-            for part in range(2):
-                w_copy(dx, dc, yb, part, me_slot).wait_send()
-    for d in range(1, 4):
-        z_copy(d, z_rows(0)).wait_send()
-    for d in range(1, CTX):
-        state_copy(d, ctx).wait_send()
+    lax.fori_loop(0, TURNS, turn, 0)
+
+    def drain_rest(u, c0):
+        drain(u, True)
+        return c0
+
+    lax.fori_loop(TURNS - 7, NC - 1, drain_rest, 0)
+    for u in range(NC - 1, NU):
+        drain(u, False)
 
 
 def on_device(key_feature, value_feature, query_gate, decay_rates, residues, skip_gain, out_weight):
@@ -392,8 +456,9 @@
             pltpu.SemaphoreType.DMA((CTX,)),
             pltpu.SemaphoreType.DMA((SLOTS, 2, 2)),
             pltpu.SemaphoreType.DMA((SLOTS, 2, 2)),
-            pltpu.SemaphoreType.DMA((4,)),
-            pltpu.SemaphoreType.DMA((4,)),
+            pltpu.SemaphoreType.DMA((5,)),
+            pltpu.SemaphoreType.DMA((5,)),
+            pltpu.SemaphoreType.REGULAR((4,)),
         ],
         compiler_params=pltpu.CompilerParams(
             collective_id=0, has_side_effects=True, vmem_limit_bytes=56 * 2**20

time: 70 us -> 65.4 us (0.934)
  Pallas kernels: 68.4 us -> 64.3 us
    pallas_call x1, Pallas kernels: 68.4 us -> 64.3 us  [on_device(): pl.pallas_call(kernel, out_shape=pltpu.VMEM((CH, TOK), bf16), in_specs=[a...]
where the time goes in v3:
time: 65.4 us; the launch traced here: 65.2 us
  Pallas kernels  64.3 us (98%)
  local copies, waits for them, and re-layouts  0.97 us (1%)
    pallas_call x1, Pallas kernels, on_device(): pl.pallas_call(kernel, out_shape=pltpu.VMEM((CH, TOK), bf16), in_specs=[a...  64.3 us

profile of v3, /device:TPU:1, one launch (start us, length us, event | category | flops | bytes accessed | tf_op | source)
XLA Modules:
  0.0 65.2 jit_solution(13355512041223737097)
XLA Ops:
  0.0 64.3 %hyena.1 = bf16[256,2048]{1,0:T(8,128)(2,1)S(1)} custom-call(bf16[256,2048]{1,0:T(8,128)(2,1)} %key_hbm.1, bf16[256,2048]{1,0:T(8,128)(2,1)} %val_hbm.1, bf16[256,2048]{1,0:T(8,128)(2,1)} %gate_hbm.1, f32[16,256]{1,0:T(8,128)} %rate_ref.1, f32[16,256]{1,0:T(8,128)} %res_ref.1, f32[1,256]{1,0:T(1,128)} %bitcast.1, bf16[256,4096]{1,0:T(8,128)(2,1)} %w_hbm.1), custom_call_target="tpu_custom_call" | custom-call | tf_op jit(solution)/shard_map/hyena/pallas_call | solution.py:428
  64.3 1.0 %copy.9 = bf16[256,2048]{1,0:T(8,128)(2,1)} copy(bf16[256,2048]{1,0:T(8,128)(2,1)S(1)} %hyena.1) | data formatting | bytes 2097152

commit v4 on v3

--- a/solution.py
+++ b/solution.py
@@ -355,7 +355,8 @@
         copy(CXP, u, full, s_next, other).wait_send()
         copy(C0, u, full, s_opp, other, 0).wait_send()
         copy(C1, u, full, s_opp, other, 1).wait_send()
-        y_copy(u, full).wait_send()
+        if full or u < NU - 1:
+            y_copy(u, full).wait_send()
 
     def drain_start():
         for dx, dc in plane:
@@ -372,10 +373,6 @@
                 state_copy(dy, dz, ctx).wait_send()
 
     def turn(i, c0):
-        @pl.when(i < NC)
-        def _():
-            conv(i)
-
         def at(lag, f, first=0, end=NU):
             u = i - lag
             for lo, hi, full in ((first, min(end, NC - 1), True), (max(first, NC - 1), end, False)):
@@ -387,7 +384,6 @@
 
         at(0, send)
         at(1, forward)
-        at(2, opposite)
 
         @pl.when(i == 1)
         def _():
@@ -401,7 +397,21 @@
         at(3, project, 2, NU)
         at(6, finish, 0, 2)
         at(5, finish, 2, NC - 1)
-        at(4, finish, NC - 1, NU)
+        at(4, finish, NC - 1, NU - 1)
+
+        @pl.when(i == TURNS - 1)
+        def _():
+            drain(NC - 2, True)
+            for u in range(NC - 1, NU):
+                drain(u, False)
+            finish(NU - 1, False)
+
+
+        @pl.when(i < NC - 1)
+        def _():
+            conv(i + 1)
+
+        at(2, opposite)
         at(7, drain, 0, TURNS - 7)
 
         @pl.when(i == 6)
@@ -410,15 +420,10 @@
 
         return c0
 
+    conv(0)
     lax.fori_loop(0, TURNS, turn, 0)
 
-    def drain_rest(u, c0):
-        drain(u, True)
-        return c0
-
-    lax.fori_loop(TURNS - 7, NC - 1, drain_rest, 0)
-    for u in range(NC - 1, NU):
-        drain(u, False)
+    y_copy(NU - 1, False).wait_send()
 
 
 def on_device(key_feature, value_feature, query_gate, decay_rates, residues, skip_gain, out_weight):

time: 65.4 us -> 63.8 us (0.976)
  Pallas kernels: 64.3 us -> 62.7 us
    pallas_call x1, Pallas kernels: 64.3 us -> 62.7 us  [on_device(): pl.pallas_call(kernel, out_shape=pltpu.VMEM((CH, TOK), bf16), in_specs=[a...]
where the time goes in v4:
time: 63.8 us; the launch traced here: 63.7 us
  Pallas kernels  62.7 us (98%)
  local copies, waits for them, and re-layouts  0.97 us (2%)
    pallas_call x1, Pallas kernels, on_device(): pl.pallas_call(kernel, out_shape=pltpu.VMEM((CH, TOK), bf16), in_specs=[a...  62.7 us

profile of v4, /device:TPU:1, one launch (start us, length us, event | category | flops | bytes accessed | tf_op | source)
XLA Modules:
  0.0 63.7 jit_solution(10197292398245155667)
XLA Ops:
  0.0 62.7 %hyena.1 = bf16[256,2048]{1,0:T(8,128)(2,1)S(1)} custom-call(bf16[256,2048]{1,0:T(8,128)(2,1)} %key_hbm.1, bf16[256,2048]{1,0:T(8,128)(2,1)} %val_hbm.1, bf16[256,2048]{1,0:T(8,128)(2,1)} %gate_hbm.1, f32[16,256]{1,0:T(8,128)} %rate_ref.1, f32[16,256]{1,0:T(8,128)} %res_ref.1, f32[1,256]{1,0:T(1,128)} %bitcast.1, bf16[256,4096]{1,0:T(8,128)(2,1)} %w_hbm.1), custom_call_target="tpu_custom_call" | custom-call | tf_op jit(solution)/shard_map/hyena/pallas_call | solution.py:433
  62.7 1.0 %copy.9 = bf16[256,2048]{1,0:T(8,128)(2,1)} copy(bf16[256,2048]{1,0:T(8,128)(2,1)S(1)} %hyena.1) | data formatting | bytes 2097152

commit v5 on v4

--- a/solution.py
+++ b/solution.py
@@ -25,7 +25,6 @@
 
 XP, XM, CO, F0, F1, CXM, CXP, C0, C1, YY = range(10)
 TURNS = NU + 4
-EARLY = 0
 
 
 def kernel(
@@ -162,7 +161,6 @@
                 gtot[n, m : m + 1, ls] = s[7:8, :]
         return c0
 
-    lax.fori_loop(0, EARLY, pass1, 0)
     pl.semaphore_wait(barrier, len(plane) + 2 + 2 * z)
     for dy in range(2):
         for dz in range(1, 4):
@@ -178,7 +176,12 @@
             for yb in range(2):
                 w_copy(dx, dc, yb, part, me_slot).start()
 
-    lax.fori_loop(EARLY, NC, pass1, 0)
+    def pass1_pair(k, c0):
+        pass1(2 * k, c0)
+        pass1(2 * k + 1, c0)
+        return c0
+
+    lax.fori_loop(0, NC // 2, pass1_pair, 0)
 
     final = jnp.zeros((MODES, CH), jnp.float32)
     for n in range(NC):
@@ -384,6 +387,7 @@
 
         at(0, send)
         at(1, forward)
+        at(2, opposite, NC - 1, NU)
 
         @pl.when(i == 1)
         def _():
@@ -411,7 +415,7 @@
         def _():
             conv(i + 1)
 
-        at(2, opposite)
+        at(2, opposite, 0, NC - 1)
         at(7, drain, 0, TURNS - 7)
 
         @pl.when(i == 6)

time: 63.8 us -> 63.2 us (level)
  no operation moved by 1% of the time
where the time goes in v5:
time: 63.2 us; the launch traced here: 63.1 us
  Pallas kernels  62.1 us (98%)
  local copies, waits for them, and re-layouts  0.97 us (2%)
    pallas_call x1, Pallas kernels, on_device(): pl.pallas_call(kernel, out_shape=pltpu.VMEM((CH, TOK), bf16), in_specs=[a...  62.1 us

profile of v5, /device:TPU:1, one launch (start us, length us, event | category | flops | bytes accessed | tf_op | source)
XLA Modules:
  0.0 63.1 jit_solution(2872060769532677584)
XLA Ops:
  0.0 62.1 %hyena.1 = bf16[256,2048]{1,0:T(8,128)(2,1)S(1)} custom-call(bf16[256,2048]{1,0:T(8,128)(2,1)} %key_hbm.1, bf16[256,2048]{1,0:T(8,128)(2,1)} %val_hbm.1, bf16[256,2048]{1,0:T(8,128)(2,1)} %gate_hbm.1, f32[16,256]{1,0:T(8,128)} %rate_ref.1, f32[16,256]{1,0:T(8,128)} %res_ref.1, f32[1,256]{1,0:T(1,128)} %bitcast.1, bf16[256,4096]{1,0:T(8,128)(2,1)} %w_hbm.1), custom_call_target="tpu_custom_call" | custom-call | tf_op jit(solution)/shard_map/hyena/pallas_call | solution.py:437
  62.1 1.0 %copy.9 = bf16[256,2048]{1,0:T(8,128)(2,1)} copy(bf16[256,2048]{1,0:T(8,128)(2,1)S(1)} %hyena.1) | data formatting | bytes 2097152
